TPU v7x, 32 devices: a whole 2x2x4 slice. The times are simulated.
32 devices in a mesh: lat: 4 (over y, x), lon: 8 (over z, core).
Axes of the slice: x: 2, y: 2, z: 4, core: 2. Of those that a mesh axis runs over, the one named last changes fastest.
Arguments:
- fine: bfloat16 [4, 48, 192, 512], P(None, 'lat', 'lon'), may hold values from -6 to 6
- fine_qkv: bfloat16 [512, 1536], replicated
- fine_out: bfloat16 [512, 512], replicated, may hold values from -0.25 to 0.25
- fine_up: bfloat16 [512, 2048], replicated, may hold values from -0.25 to 0.25
- fine_down: bfloat16 [2048, 512], replicated, may hold values from -0.125 to 0.125
- merge_weight: bfloat16 [2048, 1024], replicated, may hold values from -0.125 to 0.125
- coarse_qkv: bfloat16 [1024, 3072], replicated
- coarse_out: bfloat16 [1024, 1024], replicated, may hold values from -0.1875 to 0.1875
Outputs:
- coarse: bfloat16 [4, 24, 96, 1024], P(None, 'lat', 'lon')
All inputs are finite; a program needn't handle non-finite values.
Results may differ from a plain program's by a relative error of at most 0.02.
Values may be sent and summed in bfloat16 or wider, within the bound.
A program may use at most 192 MiB of HBM per device.

v0:
```python
import jax
import jax.numpy as jnp
from jax import lax
from jax.sharding import PartitionSpec as P

HEADS = 16
HEADS2 = 32


def extended_2(block, sides, width, periodic):
    for axis, dim in sides:
        count = lax.axis_size(axis)
        forward = [(i, i + 1) for i in range(count - 1)]
        if periodic:
            forward.append((count - 1, 0))
        backward = [(target, source) for source, target in forward]
        low = lax.ppermute(
            lax.slice_in_dim(block, block.shape[dim] - width, None, axis=dim), axis, forward
        )
        high = lax.ppermute(lax.slice_in_dim(block, 0, width, axis=dim), axis, backward)
        block = jnp.concatenate([low, block, high], axis=dim)
    return block


def normalize(values):
    values = values.astype(jnp.float32)
    center = values - jnp.mean(values, -1, keepdims=True)
    spread = jnp.mean(center * center, -1, keepdims=True)
    return center * lax.rsqrt(spread + 1e-05)


def window_band(band, valid, heads):
    levels, rows, cols, width = band.shape
    chan = width // 3
    size = chan // heads
    col_win = cols // 12
    placed = jnp.concatenate([band[1:], band[:1]], 0)
    split = placed.reshape(2, 2, 6, col_win, 12, 3, heads, size)
    windows = split.transpose(5, 0, 3, 6, 1, 2, 4, 7).reshape(3, 2 * col_win, heads, 144, size)
    scores = jnp.einsum(
        "nhqd,nhkd->nhqk", windows[0], windows[1], preferred_element_type=jnp.float32
    ) * size ** (-0.5)
    token = jnp.arange(144)
    level_in = token // 72
    lat_in = token // 12 % 6
    window_level = jnp.arange(2 * col_win) // col_win
    group = jnp.where(window_level[:, None] == 0, 0, 1 + level_in[None, :])
    keep = (group[:, :, None] == group[:, None, :]) & valid[lat_in][None, None, :]
    scores = jnp.where(keep[:, None], scores, -1e30)
    expo = jnp.exp(scores - jnp.max(scores, -1, keepdims=True))
    weights = (expo / jnp.sum(expo, -1, keepdims=True)).astype(jnp.bfloat16)
    attended = jnp.einsum(
        "nhqk,nhkd->nhqd", weights, windows[2], preferred_element_type=jnp.float32
    ).astype(jnp.bfloat16)
    attended = attended.reshape(2, col_win, heads, 2, 6, 12, size).transpose(0, 3, 4, 1, 5, 2, 6)
    attended = attended.reshape(levels, rows, cols, chan)
    return jnp.concatenate([attended[3:], attended[:3]], 0)


def local_attention(tokens, extended, w_out, heads):
    tile = tokens.shape[1]
    levels, rows, cols, width = extended.shape
    chan = width // 3
    place = lax.axis_index("lat") * tile - 3 + jnp.arange(rows)
    valid = (place >= 0) & (place < tile * lax.axis_size("lat"))
    buffer = jnp.zeros((levels, rows, cols, chan), jnp.bfloat16)

    def step(index, holder):
        start = index * 6
        band = lax.dynamic_slice_in_dim(extended, start, 6, 1)
        band_valid = lax.dynamic_slice_in_dim(valid, start, 6, 0)
        result = window_band(band, band_valid, heads)
        return lax.dynamic_update_slice_in_dim(holder, result, start, 1)

    buffer = lax.fori_loop(0, rows // 6, step, buffer)
    mixed = buffer[:, 3 : tile + 3, 6 : cols - 6]
    return tokens.astype(jnp.float32) + jnp.dot(mixed, w_out, preferred_element_type=jnp.float32)


def shards(fine, fine_qkv, fine_out, fine_up, fine_down, merge_weight, coarse_qkv, coarse_out):
    fine_norm = normalize(fine).astype(jnp.bfloat16)
    fine_proj = jnp.dot(fine_norm, fine_qkv, preferred_element_type=jnp.float32).astype(
        jnp.bfloat16
    )
    fine_wide = extended_2(fine_proj, (("lon", 2),), 6, True)
    fine_ext = extended_2(fine_wide, (("lat", 1),), 3, False)
    hidden = local_attention(fine, fine_ext, fine_out, HEADS).astype(jnp.bfloat16)
    second = normalize(hidden).astype(jnp.bfloat16)
    inner = jax.nn.gelu(
        jnp.dot(second, fine_up, preferred_element_type=jnp.float32), approximate=False
    ).astype(jnp.bfloat16)
    block = (
        hidden.astype(jnp.float32) + jnp.dot(inner, fine_down, preferred_element_type=jnp.float32)
    ).astype(jnp.bfloat16)
    levels, rows, cols, width = block.shape
    pairs = block.reshape(levels, rows // 2, 2, cols // 2, 2, width).transpose(0, 1, 3, 2, 4, 5)
    pairs = pairs.reshape(levels, rows // 2, cols // 2, 4 * width)
    merged = jnp.dot(
        normalize(pairs).astype(jnp.bfloat16), merge_weight, preferred_element_type=jnp.float32
    ).astype(jnp.bfloat16)
    coarse_norm = normalize(merged).astype(jnp.bfloat16)
    coarse_proj = jnp.dot(coarse_norm, coarse_qkv, preferred_element_type=jnp.float32).astype(
        jnp.bfloat16
    )
    coarse_wide = extended_2(coarse_proj, (("lon", 2),), 6, True)
    coarse_ext = extended_2(coarse_wide, (("lat", 1),), 3, False)
    return local_attention(merged, coarse_ext, coarse_out, HEADS2).astype(jnp.bfloat16)


def solution(mesh):
    in_specs = (P(None, "lat", "lon", None), P(), P(), P(), P(), P(), P(), P())
    out_specs = P(None, "lat", "lon", None)
    return jax.shard_map(shards, mesh=mesh, in_specs=in_specs, out_specs=out_specs, check_vma=False)
```

profile of v0, /device:TPU:0, one launch (start us, length us, event | category | flops | bytes accessed | tf_op | source)
XLA Modules:
  0.0 765.4 jit_solution(13757578418143274621)
XLA Ops:
  13.7 18.1 %collective-permute-done.1 = bf16[4,12,6,1536]{3,0,2,1:T(4,128)(2,1)S(1)} collective-permute-done((bf16[4,12,6,1536]{3,0,2,1:T(4,128)(2,1)S(1)}, bf16[4,12,6,1536]{3,0,2,1:T(4,128)(2,1)S(1)}, u32[]{:S(2)}, u32[]{:S(2)}) %collective-permute-start.1) | collective-permute-done | bytes 884768 | tf_op jit(solution)/shard_map/ppermute | solution.py:20
  46.6 25.0 %collective-permute-done.3 = bf16[4,3,36,1536]{3,0,2,1:T(4,128)(2,1)} collective-permute-done((bf16[4,3,36,1536]{3,0,2,1:T(4,128)(2,1)}, bf16[4,3,36,1536]{3,0,2,1:T(4,128)(2,1)}, u32[]{:S(2)}, u32[]{:S(2)}) %collective-permute-start.3) | collective-permute-done | bytes 1327136 | tf_op jit(solution)/shard_map/ppermute | solution.py:20
  77.5 16.6 %copy.160 = bf16[4,18,36,1536]{3,0,2,1:T(4,128)(2,1)} copy(bf16[4,18,36,1536]{3,2,1,0:T(8,128)(2,1)S(1)} %pad_maximum_fusion.2) | data formatting | bytes 15925248 | tf_op jit(solution)/shard_map/while | solution.py:75
  96.7 259.4 %while.32 = (s32[]{:T(128)}, bf16[4,18,36,512]{3,0,2,1:T(4,128)(2,1)}, pred[18]{0:T(512)(128)(4,1)S(1)}, bf16[4,18,36,1536]{3,0,2,1:T(4,128)(2,1)}, s32[]{:T(128)}, /*index=5*/s32[]{:T(128)}, s32[]{:T(128)}, s32[]{:T(128)}, s32[]{}) while((s32[]{:T(128)}, bf16[4,18,36,512]{3,0,2,1:T(4,128)(2,1)}, pred[18]{0:T(512)(128)(4,1)S(1)}, ...), condition=%wide.region_5.6_spmd, body=%wide.region_2.5_spmd.sunk | while | flops 280509184 | bytes 61981556 | solution.py:75
  111.8 12.9 %reshape.544 = bf16[2,2,6,3,12,3,16,32]{7,6,5,1,0,4,3,2:T(8,128)(2,1)} reshape(bf16[4,6,36,1536]{3,0,2,1:T(4,128)(2,1)} %pad_maximum_fusion.10) | data formatting | bytes 5308416 | tf_op jit(solution)/shard_map/while/body/eval_jaxpr/reshape | solution.py:38
  135.2 7.1 fusion.178
  142.3 9.2 %fusion.182 = f32[6,16,144]{2,1,0:T(8,128)S(1)} fusion(f32[6,16,144,144]{2,3,1,0:T(8,128)} %fusion.178, pred[6,144,144]{1,2,0:T(8,128)(4,1)S(1)} %compare_and_fusion.6), kind=kOutput, calls=%fused_computation.212.clone.1 | output fusion | flops 7962767 | bytes 8142336 | tf_op jit(solution)/shard_map/while/body/eval_jaxpr/sub | solution.py:50
  151.5 12.1 %fusion.183 = bf16[6,16,144,32]{2,3,1,0:T(8,128)(2,1)} fusion(f32[6,16,144]{2,1,0:T(8,128)S(1)} %fusion.182, bf16[6,16,144,32]{3,1,2,0:T(8,128)(2,1)} %bitcast.157, f32[6,16,144,144]{2,3,1,0:T(8,128)} %fusion.178, pred[6,144,144]{1,2,0:T(8,128)(4,1)S(1)} %compare_and_fusion.6), kind=kOutput, calls=%fused_computation.14.clone.1 | convolution fusion | flops 137811600 | bytes 9911808 | tf_op jit(solution)/shard_map/while/body/eval_jaxpr/nhqk,nhkd->nhqd/dot_general | solution.py:52
  195.5 12.9 %reshape.544 = bf16[2,2,6,3,12,3,16,32]{7,6,5,1,0,4,3,2:T(8,128)(2,1)} reshape(bf16[4,6,36,1536]{3,0,2,1:T(4,128)(2,1)} %pad_maximum_fusion.10) | data formatting | bytes 5308416 | tf_op jit(solution)/shard_map/while/body/eval_jaxpr/reshape | solution.py:38
  218.9 7.1 fusion.178
  226.0 9.2 %fusion.182 = f32[6,16,144]{2,1,0:T(8,128)S(1)} fusion(f32[6,16,144,144]{2,3,1,0:T(8,128)} %fusion.178, pred[6,144,144]{1,2,0:T(8,128)(4,1)S(1)} %compare_and_fusion.6), kind=kOutput, calls=%fused_computation.212.clone.1 | output fusion | flops 7962767 | bytes 8142336 | tf_op jit(solution)/shard_map/while/body/eval_jaxpr/sub | solution.py:50
  235.2 12.1 %fusion.183 = bf16[6,16,144,32]{2,3,1,0:T(8,128)(2,1)} fusion(f32[6,16,144]{2,1,0:T(8,128)S(1)} %fusion.182, bf16[6,16,144,32]{3,1,2,0:T(8,128)(2,1)} %bitcast.157, f32[6,16,144,144]{2,3,1,0:T(8,128)} %fusion.178, pred[6,144,144]{1,2,0:T(8,128)(4,1)S(1)} %compare_and_fusion.6), kind=kOutput, calls=%fused_computation.14.clone.1 | convolution fusion | flops 137811600 | bytes 9911808 | tf_op jit(solution)/shard_map/while/body/eval_jaxpr/nhqk,nhkd->nhqd/dot_general | solution.py:52
  279.1 12.9 %reshape.544 = bf16[2,2,6,3,12,3,16,32]{7,6,5,1,0,4,3,2:T(8,128)(2,1)} reshape(bf16[4,6,36,1536]{3,0,2,1:T(4,128)(2,1)} %pad_maximum_fusion.10) | data formatting | bytes 5308416 | tf_op jit(solution)/shard_map/while/body/eval_jaxpr/reshape | solution.py:38
  302.5 7.1 fusion.178
  309.6 9.2 %fusion.182 = f32[6,16,144]{2,1,0:T(8,128)S(1)} fusion(f32[6,16,144,144]{2,3,1,0:T(8,128)} %fusion.178, pred[6,144,144]{1,2,0:T(8,128)(4,1)S(1)} %compare_and_fusion.6), kind=kOutput, calls=%fused_computation.212.clone.1 | output fusion | flops 7962767 | bytes 8142336 | tf_op jit(solution)/shard_map/while/body/eval_jaxpr/sub | solution.py:50
  318.8 12.1 %fusion.183 = bf16[6,16,144,32]{2,3,1,0:T(8,128)(2,1)} fusion(f32[6,16,144]{2,1,0:T(8,128)S(1)} %fusion.182, bf16[6,16,144,32]{3,1,2,0:T(8,128)(2,1)} %bitcast.157, f32[6,16,144,144]{2,3,1,0:T(8,128)} %fusion.178, pred[6,144,144]{1,2,0:T(8,128)(4,1)S(1)} %compare_and_fusion.6), kind=kOutput, calls=%fused_computation.14.clone.1 | convolution fusion | flops 137811600 | bytes 9911808 | tf_op jit(solution)/shard_map/while/body/eval_jaxpr/nhqk,nhkd->nhqd/dot_general | solution.py:52
  364.7 23.5 %fusion.91 = f32[4,12,24,512]{3,2,1,0:T(8,128)} fusion(bf16[2048,512]{1,0:T(8,128)(2,1)S(1)} %copy-done.11, f32[4,12,24,2048]{3,2,1,0:T(8,128)S(1)} %get-tuple-element.351, u16[4,24,2048]{2,1,0:T(8,128)(2,1)S(1)} %get-tuple-element.304, u16[4,24,2048]{2,1,0:T(8,128)(2,1)S(1)} %get-tuple-element.303, bf16[4,12,24,512]{3,2,1,0:T(8,128)(2,1)S(1)} %get-tuple-element.350), kind=kOutput, calls=%fused_computation.157 | convolution fusion | flops 2583429120 | bytes 15859712 | tf_op jit(solution)/shard_map/dot_general | solution.py:93
  419.1 18.9 %collective-permute-done.5 = bf16[4,6,6,3072]{3,0,2,1:T(4,128)(2,1)S(1)} collective-permute-done((bf16[4,6,6,3072]{3,0,2,1:T(4,128)(2,1)S(1)}, bf16[4,6,6,3072]{3,0,2,1:T(4,128)(2,1)S(1)}, u32[]{:S(2)}, u32[]{:S(2)}) %collective-permute-start.5) | collective-permute-done | bytes 884768 | tf_op jit(solution)/shard_map/ppermute | solution.py:20
  444.6 28.2 %collective-permute-start.6 = (bf16[4,3,24,3072]{3,2,1,0:T(8,128)(2,1)}, bf16[4,3,24,3072]{3,2,1,0:T(8,128)(2,1)}, u32[]{:S(2)}, u32[]{:S(2)}) collective-permute-start(bf16[4,3,24,3072]{3,2,1,0:T(8,128)(2,1)} %get-tuple-element.343), channel_id=1, source_target_pairs={{0,8},{8,16},{16,24},{1,9},{9,17},{17,25},{2,10},{10,18},{18,26},{... | collective-permute-start | bytes 5308424 | tf_op jit(solution)/shard_map/ppermute | solution.py:17
  474.1 28.8 %collective-permute-done.6 = bf16[4,3,24,3072]{3,2,1,0:T(8,128)(2,1)} collective-permute-done((bf16[4,3,24,3072]{3,2,1,0:T(8,128)(2,1)}, bf16[4,3,24,3072]{3,2,1,0:T(8,128)(2,1)}, u32[]{:S(2)}, u32[]{:S(2)}) %collective-permute-start.6) | collective-permute-done | bytes 1769504 | tf_op jit(solution)/shard_map/ppermute | solution.py:17
  503.0 41.7 %collective-permute-done.7 = bf16[4,3,24,3072]{3,2,1,0:T(8,128)(2,1)} collective-permute-done((bf16[4,3,24,3072]{3,2,1,0:T(8,128)(2,1)}, bf16[4,3,24,3072]{3,2,1,0:T(8,128)(2,1)}, u32[]{:S(2)}, u32[]{:S(2)}) %collective-permute-start.7) | collective-permute-done | bytes 1769504 | tf_op jit(solution)/shard_map/ppermute | solution.py:20
  553.0 207.8 %while.33 = (s32[]{:T(128)}, bf16[4,12,24,1024]{3,2,1,0:T(8,128)(2,1)}, pred[12]{0:T(512)(128)(4,1)S(1)}, bf16[4,12,24,3072]{3,2,1,0:T(8,128)(2,1)}, s32[]{:T(128)}, /*index=5*/s32[]{:T(128)}, s32[]{:T(128)}, s32[]{:T(128)}, s32[]{}) while((s32[]{:T(128)}, bf16[4,12,24,1024]{3,2,1,0:T(8,128)(2,1)}, pred[12]{0:T(512)(128)(4,1)S(1)}, ...), condition=%wide.region_15.16_spmd, body=%wide.region_12.15_spmd.sunk | while | flops 365862720 | bytes 94691440 | solution.py:75
  563.3 16.2 %reshape.546 = bf16[2,2,6,2,12,3,32,32]{7,6,5,4,3,2,1,0:T(8,128)(2,1)} reshape(bf16[4,6,24,3072]{3,2,1,0:T(8,128)(2,1)} %pad_maximum_fusion.11) | data formatting | bytes 7077888 | tf_op jit(solution)/shard_map/while/body/eval_jaxpr/reshape | solution.py:38
  579.5 7.4 copy.246
  593.0 13.5 %fusion.188 = f32[4,32,144,144]{2,3,1,0:T(8,128)} fusion(bf16[4,32,144,32]{3,1,2,0:T(8,128)(2,1)} %bitcast.149, bf16[4,32,144,32]{3,1,2,0:T(8,128)(2,1)} %bitcast.150), kind=kOutput, calls=%fused_computation.54.clone.1 | convolution fusion | flops 169869312 | bytes 12976128 | tf_op jit(solution)/shard_map/while/body/eval_jaxpr/nhqd,nhkd->nhqk/dot_general | solution.py:40
  606.5 20.4 %fusion.192 = (f32[4,32,144]{2,1,0:T(8,128)S(1)}, f32[4,32,144,144]{2,3,1,0:T(8,128)}) fusion(f32[4,32,144,144]{2,3,1,0:T(8,128)} %fusion.188, pred[4,144,144]{1,2,0:T(8,128)(4,1)S(1)} %compare_and_fusion.7), kind=kOutput, calls=%fused_computation.215.clone.1 | output fusion | flops 15925391 | bytes 21390336 | tf_op jit(solution)/shard_map/while/body/eval_jaxpr/sub | solution.py:50
  626.9 10.4 %fusion.193 = bf16[4,32,144,32]{2,3,1,0:T(8,128)(2,1)S(1)} fusion(f32[4,32,144,144]{2,3,1,0:T(8,128)} %get-tuple-element.441, f32[4,32,144]{2,1,0:T(8,128)S(1)} %get-tuple-element.442, bf16[4,32,144,32]{3,1,2,0:T(8,128)(2,1)} %bitcast.156), kind=kOutput, calls=%fused_computation.58.clone.1 | convolution fusion | flops 175767552 | bytes 13049856 | tf_op jit(solution)/shard_map/while/body/eval_jaxpr/nhqk,nhkd->nhqd/dot_general | solution.py:52
  667.1 16.2 %reshape.546 = bf16[2,2,6,2,12,3,32,32]{7,6,5,4,3,2,1,0:T(8,128)(2,1)} reshape(bf16[4,6,24,3072]{3,2,1,0:T(8,128)(2,1)} %pad_maximum_fusion.11) | data formatting | bytes 7077888 | tf_op jit(solution)/shard_map/while/body/eval_jaxpr/reshape | solution.py:38
  683.3 7.4 copy.246
  696.8 13.5 %fusion.188 = f32[4,32,144,144]{2,3,1,0:T(8,128)} fusion(bf16[4,32,144,32]{3,1,2,0:T(8,128)(2,1)} %bitcast.149, bf16[4,32,144,32]{3,1,2,0:T(8,128)(2,1)} %bitcast.150), kind=kOutput, calls=%fused_computation.54.clone.1 | convolution fusion | flops 169869312 | bytes 12976128 | tf_op jit(solution)/shard_map/while/body/eval_jaxpr/nhqd,nhkd->nhqk/dot_general | solution.py:40
  710.3 20.4 %fusion.192 = (f32[4,32,144]{2,1,0:T(8,128)S(1)}, f32[4,32,144,144]{2,3,1,0:T(8,128)}) fusion(f32[4,32,144,144]{2,3,1,0:T(8,128)} %fusion.188, pred[4,144,144]{1,2,0:T(8,128)(4,1)S(1)} %compare_and_fusion.7), kind=kOutput, calls=%fused_computation.215.clone.1 | output fusion | flops 15925391 | bytes 21390336 | tf_op jit(solution)/shard_map/while/body/eval_jaxpr/sub | solution.py:50
  730.7 10.4 %fusion.193 = bf16[4,32,144,32]{2,3,1,0:T(8,128)(2,1)S(1)} fusion(f32[4,32,144,144]{2,3,1,0:T(8,128)} %get-tuple-element.441, f32[4,32,144]{2,1,0:T(8,128)S(1)} %get-tuple-element.442, bf16[4,32,144,32]{3,1,2,0:T(8,128)(2,1)} %bitcast.156), kind=kOutput, calls=%fused_computation.58.clone.1 | convolution fusion | flops 175767552 | bytes 13049856 | tf_op jit(solution)/shard_map/while/body/eval_jaxpr/nhqk,nhkd->nhqd/dot_general | solution.py:52
  (181 shorter events, 295.1 us)
Async XLA Ops:
  0.0 360.3 %copy-start = (bf16[512,2048]{1,0:T(8,128)(2,1)S(1)}, bf16[512,2048]{1,0:T(8,128)(2,1)}, u32[]{:S(2)}) copy-start(bf16[512,2048]{1,0:T(8,128)(2,1)} %param.15) | copy-start | bytes 6291460
  7.4 26.8 %copy-start.3 = (bf16[4,12,24,1536]{3,2,1,0:T(8,128)(2,1)}, bf16[4,12,24,1536]{3,2,1,0:T(8,128)(2,1)S(1)}, u32[]{:S(2)}) copy-start(bf16[4,12,24,1536]{3,2,1,0:T(8,128)(2,1)S(1)} %convolution_convert_fusion) | copy-start | bytes 10616836
  8.4 23.4 %collective-permute-start.1 = (bf16[4,12,6,1536]{3,0,2,1:T(4,128)(2,1)S(1)}, bf16[4,12,6,1536]{3,0,2,1:T(4,128)(2,1)S(1)}, u32[]{:S(2)}, u32[]{:S(2)}) collective-permute-start(bf16[4,12,6,1536]{3,0,2,1:T(4,128)(2,1)S(1)} %copy.153), channel_id=1, source_target_pairs={{1,0},{2,1},{3,2},{4,3},{5,4},{6,5},{7,6},{0,7},{9,8},{10,9},{11,1... | collective-permute-start | bytes 2654216 | tf_op jit(solution)/shard_map/ppermute | solution.py:20
  13.6 20.4 %collective-permute-start = (bf16[4,12,6,1536]{3,0,2,1:T(4,128)(2,1)S(1)}, bf16[4,12,6,1536]{3,0,2,1:T(4,128)(2,1)S(1)}, u32[]{:S(2)}, u32[]{:S(2)}) collective-permute-start(bf16[4,12,6,1536]{3,0,2,1:T(4,128)(2,1)S(1)} %copy.152), channel_id=1, source_target_pairs={{0,1},{1,2},{2,3},{3,4},{4,5},{5,6},{6,7},{7,0},{8,9},{9,10},{10,1... | collective-permute-start | bytes 2654216 | tf_op jit(solution)/shard_map/ppermute | solution.py:17
  34.2 1.4 copy-start.6
  37.4 34.3 %collective-permute-start.3 = (bf16[4,3,36,1536]{3,0,2,1:T(4,128)(2,1)}, bf16[4,3,36,1536]{3,0,2,1:T(4,128)(2,1)}, u32[]{:S(2)}, u32[]{:S(2)}) collective-permute-start(bf16[4,3,36,1536]{3,0,2,1:T(4,128)(2,1)} %copy.157), channel_id=1, source_target_pairs={{8,0},{16,8},{24,16},{9,1},{17,9},{25,17},{10,2},{18,10},{26,18},{... | collective-permute-start | bytes 3981320 | tf_op jit(solution)/shard_map/ppermute | solution.py:20
  40.4 32.8 %collective-permute-start.2 = (bf16[4,3,36,1536]{3,0,2,1:T(4,128)(2,1)}, bf16[4,3,36,1536]{3,0,2,1:T(4,128)(2,1)}, u32[]{:S(2)}, u32[]{:S(2)}) collective-permute-start(bf16[4,3,36,1536]{3,0,2,1:T(4,128)(2,1)} %copy.156), channel_id=1, source_target_pairs={{0,8},{8,16},{16,24},{1,9},{9,17},{17,25},{2,10},{10,18},{18,26},{... | collective-permute-start | bytes 3981320 | tf_op jit(solution)/shard_map/ppermute | solution.py:17
  46.6 28.2 %copy-start.4 = (bf16[4,12,24,1536]{3,2,1,0:T(8,128)(2,1)S(1)}, bf16[4,12,24,1536]{3,2,1,0:T(8,128)(2,1)}, u32[]{:S(2)}) copy-start(bf16[4,12,24,1536]{3,2,1,0:T(8,128)(2,1)} %copy-done.3) | copy-start | bytes 10616836
  46.6 28.2 %copy-start.7 = (bf16[4,12,6,1536]{3,2,1,0:T(8,128)(2,1)S(1)}, bf16[4,12,6,1536]{3,2,1,0:T(8,128)(2,1)}, u32[]{:S(2)}) copy-start(bf16[4,12,6,1536]{3,2,1,0:T(8,128)(2,1)} %copy-done.6) | copy-start | bytes 2654212
  356.1 2.5 copy-start.8
  356.2 2.5 copy-start.12
  360.3 4.4 copy-start.11
  392.4 7.0 copy-start.2
  405.8 7.2 slice-start
  408.3 4.7 slice-start.1
  412.6 3.6 copy-start.9
  416.2 24.5 %copy-start.5 = (bf16[4,6,12,3072]{3,2,1,0:T(8,128)(2,1)}, bf16[4,6,12,3072]{3,2,1,0:T(8,128)(2,1)S(1)}, u32[]{:S(2)}) copy-start(bf16[4,6,12,3072]{3,2,1,0:T(8,128)(2,1)S(1)} %fusion.56) | copy-start | bytes 5308420
  417.4 20.7 %collective-permute-start.5 = (bf16[4,6,6,3072]{3,0,2,1:T(4,128)(2,1)S(1)}, bf16[4,6,6,3072]{3,0,2,1:T(4,128)(2,1)S(1)}, u32[]{:S(2)}, u32[]{:S(2)}) collective-permute-start(bf16[4,6,6,3072]{3,0,2,1:T(4,128)(2,1)S(1)} %copy.174), channel_id=1, source_target_pairs={{1,0},{2,1},{3,2},{4,3},{5,4},{6,5},{7,6},{0,7},{9,8},{10,9},{11,1... | collective-permute-start | bytes 2654216 | tf_op jit(solution)/shard_map/ppermute | solution.py:20
  419.0 21.4 %collective-permute-start.4 = (bf16[4,6,6,3072]{3,0,2,1:T(4,128)(2,1)S(1)}, bf16[4,6,6,3072]{3,0,2,1:T(4,128)(2,1)S(1)}, u32[]{:S(2)}, u32[]{:S(2)}) collective-permute-start(bf16[4,6,6,3072]{3,0,2,1:T(4,128)(2,1)S(1)} %copy.173), channel_id=1, source_target_pairs={{0,1},{1,2},{2,3},{3,4},{4,5},{5,6},{6,7},{7,0},{8,9},{9,10},{10,1... | collective-permute-start | bytes 2654216 | tf_op jit(solution)/shard_map/ppermute | solution.py:17
  444.6 58.3 %collective-permute-start.6 = (bf16[4,3,24,3072]{3,2,1,0:T(8,128)(2,1)}, bf16[4,3,24,3072]{3,2,1,0:T(8,128)(2,1)}, u32[]{:S(2)}, u32[]{:S(2)}) collective-permute-start(bf16[4,3,24,3072]{3,2,1,0:T(8,128)(2,1)} %get-tuple-element.343), channel_id=1, source_target_pairs={{0,8},{8,16},{16,24},{1,9},{9,17},{17,25},{2,10},{10,18},{18,26},{... | collective-permute-start | bytes 5308424 | tf_op jit(solution)/shard_map/ppermute | solution.py:17
  472.8 71.8 %collective-permute-start.7 = (bf16[4,3,24,3072]{3,2,1,0:T(8,128)(2,1)}, bf16[4,3,24,3072]{3,2,1,0:T(8,128)(2,1)}, u32[]{:S(2)}, u32[]{:S(2)}) collective-permute-start(bf16[4,3,24,3072]{3,2,1,0:T(8,128)(2,1)} %get-tuple-element.344), channel_id=1, source_target_pairs={{8,0},{16,8},{24,16},{9,1},{17,9},{25,17},{10,2},{18,10},{26,18},{... | collective-permute-start | bytes 5308424 | tf_op jit(solution)/shard_map/ppermute | solution.py:20
  553.0 207.8 %copy-start.10 = (bf16[4,6,12,1024]{3,2,1,0:T(8,128)(2,1)S(1)}, bf16[4,6,12,1024]{3,2,1,0:T(8,128)(2,1)}, u32[]{:S(2)}) copy-start(bf16[4,6,12,1024]{3,2,1,0:T(8,128)(2,1)} %copy-done.9) | copy-start | bytes 1769476
  760.8 4.4 copy-start.1
where the time goes:
time: 778 us; the launch traced here: 765 us
  local copies, waits for them, and re-layouts  291 us (37%)
  matrix products  149 us (19%)
  other arithmetic  137 us (18%)
  waiting for transfers between devices  137 us (18%)
  starting transfers between devices  42.5 us (5%)
  loops' own time  8.97 us (1%)
    ppermute x4, waiting for transfers between devices, extended_2(): lax.ppermute(lax.slice_in_dim(block, 0, width, axis=dim), axis, backward)  104 us
    reshape x7, local copies, waits for them, and re-layouts, window_band(): split = placed.reshape(2, 2, 6, col_win, 12, 3, heads, size)  86.1 us
    sub x5, other arithmetic, window_band(): expo = jnp.exp(scores - jnp.max(scores, -1, keepdims=True))  68.5 us
    dot_general x5, matrix products, window_band(): jnp.einsum('nhqk,nhkd->nhqd', weights, windows[2], preferred_element_type...  57.1 us
    dot_general x5, matrix products, window_band(): jnp.einsum('nhqd,nhkd->nhqk', windows[0], windows[1], preferred_element_t...  48.1 us
    slice x8, local copies, waits for them, and re-layouts, window_band(): windows[2]  37.4 us
    ppermute x4, starting transfers between devices, extended_2(): lax.ppermute(lax.slice_in_dim(block, block.shape[dim] - width, None, axis...  34.4 us
    ppermute x4, waiting for transfers between devices, extended_2(): lax.ppermute(lax.slice_in_dim(block, block.shape[dim] - width, None, axis...  33 us
  transfers between devices with their start and end apart: 8, of which 7 were waited for; matrix products, arithmetic and copies ran while one was open for 1% of the time, Pallas kernels for 0%

commit v1 on v0

v1 whole, which is shorter than its diff:
```python
import functools

import numpy as np
import jax
import jax.numpy as jnp
from jax import lax
from jax.experimental import pallas as pl
from jax.experimental.pallas import tpu as pltpu
from jax.sharding import PartitionSpec as P

HEADS = 16
HEADS2 = 32
ROWS = 3
COLS = 12
SEG = 2 * ROWS * COLS
LEVEL = ROWS * COLS
LANES = 128
F32 = jnp.float32
BF16 = jnp.bfloat16


def normalize(values):
    center = values - jnp.mean(values, -1, keepdims=True)
    spread = jnp.mean(center * center, -1, keepdims=True)
    return center * lax.rsqrt(spread + 1e-05)


def matmul(a, b):
    return jnp.dot(a, b, preferred_element_type=F32)


def attend(q_ref, kv_ref, out_ref, pair, lat, last, segs, heads, chan):
    size = chan // heads
    per = LANES // size
    windows = (segs + 2) // 2
    key = lax.broadcasted_iota(jnp.int32, (SEG, 2 * SEG), 1)
    query = lax.broadcasted_iota(jnp.int32, (SEG, 2 * SEG), 0)
    apart = ((key // LEVEL) % 2 != query // LEVEL) & (pair == 1)
    bias = jnp.where(apart, -1e30, 0.0)
    first = jnp.where(lat == 0, -1e30, 0.0)
    final = jnp.where(lat == last, -1e30, 0.0)
    top = jnp.minimum(bias, jnp.where(key < SEG, first, 0.0))
    bottom = jnp.minimum(bias, jnp.where(key >= SEG, final, 0.0))
    head_of = lax.broadcasted_iota(jnp.int32, (1, LANES), 1) // size
    ones = jnp.ones((2 * SEG, LANES), BF16)

    def group(g, carry):
        lane = pl.multiple_of(g * LANES, LANES)
        for w in range(windows):
            rows = pl.ds(2 * w * SEG, 2 * SEG)
            keys = kv_ref[rows, pl.ds(lane, LANES)]
            values = kv_ref[rows, pl.ds(pl.multiple_of(chan + lane, LANES), LANES)]
            values = jnp.concatenate([values, ones], 1)
            for s in (2 * w - 1, 2 * w):
                if s < 0 or s >= segs:
                    continue
                shut = top if w == 0 else bottom if w == windows - 1 else bias
                mine = pl.ds(s * SEG, SEG)
                q = q_ref[mine, pl.ds(lane, LANES)]
                total = jnp.zeros((SEG, LANES), F32)
                for h in range(per):
                    q_h = jnp.where(head_of == h, q, 0.0).astype(BF16)
                    scores = lax.dot_general(
                        q_h, keys, (((1,), (1,)), ((), ())), preferred_element_type=F32
                    ) + shut
                    expo = jnp.exp(scores - jnp.max(scores, -1, keepdims=True)).astype(BF16)
                    both = matmul(expo, values)
                    total = jnp.where(head_of == h, both[:, :LANES] / both[:, LANES:], total)
                out_ref[mine, pl.ds(lane, LANES)] = total
        return carry

    lax.fori_loop(0, chan // LANES, group, 0)


def project(x, w_ref, q_ref, kv_ref, heads, chan):
    own = q_ref.shape[0]
    normed = normalize(x)
    kv_ref[...] = matmul(normed.astype(BF16), w_ref[:, chan:]).astype(BF16)
    q_ref[...] = matmul(normed[SEG : SEG + own].astype(BF16), w_ref[:, :chan]) * (
        (chan // heads) ** -0.5
    )


def fine_kernel(col_win, x_ref, qkv_ref, out_ref, up_ref, down_ref, merge_ref, pick_ref, merged_ref,
                q_ref, kv_ref, att_ref):
    lat, last = lax.axis_index("lat"), lax.axis_size("lat") - 1
    own, chan = q_ref.shape
    x = x_ref[0].astype(F32)
    project(x, qkv_ref, q_ref, kv_ref, HEADS, chan)
    pair = pl.program_id(0) // col_win
    attend(q_ref, kv_ref, att_ref, pair, lat, last, own // SEG, HEADS, chan)
    mixed = matmul(att_ref[...].astype(BF16), out_ref[...])
    hidden = (x[SEG : SEG + own] + mixed).astype(BF16).astype(F32)
    second = normalize(hidden).astype(BF16)
    block = hidden
    width = up_ref.shape[1]
    step = 512
    for start in range(0, width, step):
        part = matmul(second, up_ref[:, start : start + step])
        inner = 0.5 * part * (1.0 + lax.erf(part * (0.5 ** 0.5)))
        block = block + matmul(inner.astype(BF16), down_ref[start : start + step, :])
    quads = matmul(pick_ref[...], block.astype(BF16))
    count = own // 4
    quads = [quads[i * count : (i + 1) * count] for i in range(4)]
    mean = sum(jnp.sum(part, -1, keepdims=True) for part in quads) / (4 * chan)
    quads = [part - mean for part in quads]
    spread = sum(jnp.sum(part * part, -1, keepdims=True) for part in quads) / (4 * chan)
    scale = lax.rsqrt(spread + 1e-05)
    merged = sum(
        matmul((part * scale).astype(BF16), merge_ref[i * chan : (i + 1) * chan, :])
        for i, part in enumerate(quads)
    )
    merged_ref[0] = merged.astype(BF16)


def coarse_kernel(x_ref, qkv_ref, out_ref, res_ref, q_ref, kv_ref, att_ref):
    lat, last = lax.axis_index("lat"), lax.axis_size("lat") - 1
    own, chan = q_ref.shape
    x = x_ref[0].astype(F32)
    project(x, qkv_ref, q_ref, kv_ref, HEADS2, chan)
    attend(q_ref, kv_ref, att_ref, pl.program_id(0), lat, last, own // SEG, HEADS2, chan)
    mixed = matmul(att_ref[...].astype(BF16), out_ref[...])
    res_ref[0] = (x[SEG : SEG + own] + mixed).astype(BF16)


def call(kernel, ext, weights, out_rows, out_width, chan, flops):
    steps, rows, width = ext.shape
    own = rows - 2 * SEG
    whole = [
        pl.BlockSpec(w.shape, lambda i: (0, 0), pipeline_mode=pl.Buffered(1)) for w in weights
    ]
    return pl.pallas_call(
        kernel,
        grid=(steps,),
        in_specs=[pl.BlockSpec((1, rows, width), lambda i: (i, 0, 0))] + whole,
        out_specs=pl.BlockSpec((1, out_rows, out_width), lambda i: (i, 0, 0)),
        out_shape=jax.ShapeDtypeStruct((steps, out_rows, out_width), BF16),
        scratch_shapes=[
            pltpu.VMEM((own, chan), F32),
            pltpu.VMEM((rows, 2 * chan), BF16),
            pltpu.VMEM((own, chan), F32),
        ],
        compiler_params=pltpu.CompilerParams(vmem_limit_bytes=48 * 2**20),
        cost_estimate=pl.CostEstimate(flops=flops, bytes_accessed=20 * 2**20, transcendentals=0),
    )(ext, *weights)


def from_next(block, axis, periodic):
    count = lax.axis_size(axis)
    pairs = [(i, i - 1) for i in range(1, count)] + ([(0, count - 1)] if periodic else [])
    return lax.ppermute(block, axis, pairs)


def from_last(block, axis, periodic):
    count = lax.axis_size(axis)
    pairs = [(i, i + 1) for i in range(count - 1)] + ([(count - 1, 0)] if periodic else [])
    return lax.ppermute(block, axis, pairs)


def widen(segments):
    low = from_last(segments[:, -1:], "lat", False)
    high = from_next(segments[:, :1], "lat", False)
    ext = jnp.concatenate([low, segments, high], 1)
    return ext.reshape(ext.shape[0], -1, ext.shape[-1])


def pick_matrix(rows):
    half = COLS // 2
    count = 2 * (rows // 2) * half
    pick = np.zeros((4 * count, 4 * count), np.float32)
    for quad in range(4):
        for r in range(count):
            level, i, j = r // (rows // 2 * half), r // half % (rows // 2), r % half
            row, col = 2 * i + quad // 2, 2 * j + quad % 2
            pick[quad * count + r, row // ROWS * SEG + level * LEVEL + row % ROWS * COLS + col] = 1
    return pick


def shards(fine, fine_qkv, fine_out, fine_up, fine_down, merge_weight, coarse_qkv, coarse_out):
    levels, rows, cols, chan = fine.shape
    col_win = cols // COLS
    shifted = jnp.concatenate([fine[:, :, 6:], from_next(fine[:, :, :6], "lon", True)], 2)
    placed = jnp.concatenate([shifted[1:], shifted[:1]], 0)
    split = placed.reshape(2, 2, rows // ROWS, ROWS, col_win, COLS, chan)
    segments = split.transpose(0, 4, 2, 1, 3, 5, 6).reshape(2 * col_win, rows // ROWS, SEG, chan)
    pick = jnp.asarray(pick_matrix(rows), BF16)
    wide = merge_weight.shape[1]
    merged = call(
        functools.partial(fine_kernel, col_win), widen(segments),
        (fine_qkv, fine_out, fine_up, fine_down, merge_weight, pick),
        rows * COLS // 2, wide, chan, 14 * 10**9,
    )
    rows2, cols2 = rows // 2, cols // 2
    merged = merged.reshape(2, col_win, 2, rows2, COLS // 2, wide).transpose(0, 2, 3, 1, 4, 5)
    merged = merged.reshape(levels, rows2, cols2, wide)
    merged = jnp.concatenate([merged[:, :, 3:], from_next(merged[:, :, :3], "lon", True)], 2)
    win2 = cols2 // COLS
    split = merged.reshape(2, 2, rows2 // ROWS, ROWS, win2, COLS, wide)
    segments = split.transpose(0, 4, 2, 1, 3, 5, 6).reshape(2 * win2, rows2 // ROWS, SEG, wide)
    coarse = call(
        coarse_kernel, widen(segments), (coarse_qkv, coarse_out),
        rows2 * 2 * COLS, wide, wide, 7 * 10**9,
    )
    coarse = coarse.reshape(2, win2, rows2 // ROWS, 2, ROWS, COLS, wide)
    coarse = coarse.transpose(0, 3, 2, 4, 1, 5, 6).reshape(levels, rows2, cols2, wide)
    coarse = jnp.concatenate([coarse[3:], coarse[:3]], 0)
    moved = from_last(coarse[:, :, cols2 - 6 :], "lon", True)
    return jnp.concatenate([moved, coarse[:, :, : cols2 - 6]], 2)


def solution(mesh):
    in_specs = (P(None, "lat", "lon", None), P(), P(), P(), P(), P(), P(), P())
    out_specs = P(None, "lat", "lon", None)
    return jax.shard_map(shards, mesh=mesh, in_specs=in_specs, out_specs=out_specs, check_vma=False)
```

time: 778 us -> 192 us (0.25)
  the two profiles are of different devices: /device:TPU:0 before, /device:TPU:6 now
where the time goes in v1:
time: 192 us; the launch traced here: 191 us
  Pallas kernels  120 us (62%)
  waiting for transfers between devices  34.9 us (18%)
  local copies, waits for them, and re-layouts  16.3 us (8%)
  starting transfers between devices  13.2 us (7%)
  other arithmetic  6.18 us (3%)
    pallas_call x2, Pallas kernels, call(): pl.pallas_call(kernel, grid=(steps,), in_specs=[pl.BlockSpec((1, rows, wi...  120 us
    ppermute x3, waiting for transfers between devices, from_last(): return lax.ppermute(block, axis, pairs)  22.3 us
    ppermute x4, waiting for transfers between devices, from_next(): return lax.ppermute(block, axis, pairs)  12.6 us
    ppermute x4, starting transfers between devices, from_next(): return lax.ppermute(block, axis, pairs)  10.4 us
    concatenate x2, other arithmetic, widen(): ext = jnp.concatenate([low, segments, high], 1)  3.94 us
  transfers between devices with their start and end apart: 7, of which 7 were waited for; matrix products, arithmetic and copies ran while one was open for 2% of the time, Pallas kernels for 0%

profile of v1, /device:TPU:6, one launch (start us, length us, event | category | flops | bytes accessed | tf_op | source)
XLA Modules:
  0.0 191.3 jit_solution(17595092300765429255)
XLA Ops:
  0.0 1.0 slice.43
  1.0 3.1 %collective-permute-start = (bf16[4,12,6,512]{3,2,1,0:T(8,128)(2,1)S(1)}, bf16[4,12,6,512]{3,2,1,0:T(8,128)(2,1)S(1)}, u32[]{:S(2)}, u32[]{:S(2)}) collective-permute-start(bf16[4,12,6,512]{3,2,1,0:T(8,128)(2,1)S(1)} %slice.43), channel_id=1, source_target_pairs={{1,0},{2,1},{3,2},{4,3},{5,4},{6,5},{7,6},{0,7},{9,8},{10,9},{11,1... | collective-permute-start | bytes 884744 | tf_op jit(solution)/shard_map/ppermute | solution.py:151
  4.1 1.8 slice.42
  5.9 3.5 %collective-permute-done = bf16[4,12,6,512]{3,2,1,0:T(8,128)(2,1)S(1)} collective-permute-done((bf16[4,12,6,512]{3,2,1,0:T(8,128)(2,1)S(1)}, bf16[4,12,6,512]{3,2,1,0:T(8,128)(2,1)S(1)}, u32[]{:S(2)}, u32[]{:S(2)}) %collective-permute-start) | collective-permute-done | bytes 294944 | tf_op jit(solution)/shard_map/ppermute | solution.py:151
  9.7 0.9 copy.29
  10.6 0.5 reshape.30
  11.1 0.9 copy.30
  12.1 0.8 fusion.4
  12.9 2.5 %collective-permute-start.2 = (bf16[4,1,72,512]{3,2,1,0:T(8,128)(2,1)S(1)}, bf16[4,1,72,512]{3,2,1,0:T(8,128)(2,1)S(1)}, u32[]{:S(2)}, u32[]{:S(2)}) collective-permute-start(bf16[4,1,72,512]{3,2,1,0:T(8,128)(2,1)S(1)} %copy.32), channel_id=1, source_target_pairs={{8,0},{16,8},{24,16},{9,1},{17,9},{25,17},{10,2},{18,10},{26,18},{... | collective-permute-start | bytes 884744 | tf_op jit(solution)/shard_map/ppermute | solution.py:151
  15.4 1.5 collective-permute-start.1
  16.9 3.7 %collective-permute-done.2 = bf16[4,1,72,512]{3,2,1,0:T(8,128)(2,1)S(1)} collective-permute-done((bf16[4,1,72,512]{3,2,1,0:T(8,128)(2,1)S(1)}, bf16[4,1,72,512]{3,2,1,0:T(8,128)(2,1)S(1)}, u32[]{:S(2)}, u32[]{:S(2)}) %collective-permute-start.2) | collective-permute-done | bytes 294944 | tf_op jit(solution)/shard_map/ppermute | solution.py:151
  21.1 7.7 %collective-permute-done.1 = bf16[4,1,72,512]{3,2,1,0:T(8,128)(2,1)S(1)} collective-permute-done((bf16[4,1,72,512]{3,2,1,0:T(8,128)(2,1)S(1)}, bf16[4,1,72,512]{3,2,1,0:T(8,128)(2,1)S(1)}, u32[]{:S(2)}, u32[]{:S(2)}) %collective-permute-start.1) | collective-permute-done | bytes 294944 | tf_op jit(solution)/shard_map/ppermute | solution.py:157
  29.3 2.0 %pad_maximum_fusion = bf16[4,6,72,512]{3,1,2,0:T(8,128)(2,1)S(1)} fusion(bf16[4,1,72,512]{3,1,2,0:T(2,128)(2,1)S(1)} %copy.34, bf16[4,4,72,512]{3,1,2,0:T(4,128)(2,1)S(1)} %bitcast.24, bf16[4,1,72,512]{3,1,2,0:T(2,128)(2,1)S(1)} %copy.33), kind=kLoop, calls=%fused_computation | loop fusion | flops 5308416 | bytes 3538944 | tf_op jit(solution)/shard_map/concatenate | solution.py:163
  31.3 0.6 copy.35
  31.9 0.8 copy-done.1
  32.8 82.6 %shard_map.91 = bf16[4,72,1024]{2,1,0:T(8,128)(2,1)S(1)} custom-call(bf16[4,432,512]{2,1,0:T(8,128)(2,1)S(1)} %bitcast.21, bf16[512,1536]{1,0:T(8,128)(2,1)S(1)} %copy-done.1, bf16[512,512]{1,0:T(8,128)(2,1)S(1)} %copy-done.2, bf16[512,2048]{1,0:T(8,128)(2,1)} %up_ref.1, bf16[2048,512]{1,0:T(8,128)(2,1)} %down_ref.1, bf16[2048,1024]{1,0:T(8,128)(2,1)} %merge_ref.1, ...), custom_call_target="tpu_custom_call" | custom-call | flops 14000000000 | bytes 20971520 | tf_op jit(solution)/shard_map/pallas_call | solution.py:132
  116.1 0.6 copy.37
  117.0 2.4 %collective-permute-start.3 = (bf16[4,6,3,1024]{3,0,2,1:T(4,128)(2,1)S(1)}, bf16[4,6,3,1024]{3,0,2,1:T(4,128)(2,1)S(1)}, u32[]{:S(2)}, u32[]{:S(2)}) collective-permute-start(bf16[4,6,3,1024]{3,0,2,1:T(4,128)(2,1)S(1)} %slice.61), channel_id=1, source_target_pairs={{1,0},{2,1},{3,2},{4,3},{5,4},{6,5},{7,6},{0,7},{9,8},{10,9},{11,1... | collective-permute-start | bytes 442376 | tf_op jit(solution)/shard_map/ppermute | solution.py:151
  119.6 2.5 %collective-permute-done.3 = bf16[4,6,3,1024]{3,0,2,1:T(4,128)(2,1)S(1)} collective-permute-done((bf16[4,6,3,1024]{3,0,2,1:T(4,128)(2,1)S(1)}, bf16[4,6,3,1024]{3,0,2,1:T(4,128)(2,1)S(1)}, u32[]{:S(2)}, u32[]{:S(2)}) %collective-permute-start.3) | collective-permute-done | bytes 147488 | tf_op jit(solution)/shard_map/ppermute | solution.py:151
  122.7 0.6 copy.38
  123.3 0.8 fusion.5
  124.3 2.5 %collective-permute-start.5 = (bf16[2,1,72,1024]{3,2,1,0:T(8,128)(2,1)S(1)}, bf16[2,1,72,1024]{3,2,1,0:T(8,128)(2,1)S(1)}, u32[]{:S(2)}, u32[]{:S(2)}) collective-permute-start(bf16[2,1,72,1024]{3,2,1,0:T(8,128)(2,1)S(1)} %copy.40), channel_id=1, source_target_pairs={{8,0},{16,8},{24,16},{9,1},{17,9},{25,17},{10,2},{18,10},{26,18},{... | collective-permute-start | bytes 884744 | tf_op jit(solution)/shard_map/ppermute | solution.py:151
  126.8 1.3 collective-permute-start.4
  128.1 2.9 %collective-permute-done.5 = bf16[2,1,72,1024]{3,2,1,0:T(8,128)(2,1)S(1)} collective-permute-done((bf16[2,1,72,1024]{3,2,1,0:T(8,128)(2,1)S(1)}, bf16[2,1,72,1024]{3,2,1,0:T(8,128)(2,1)S(1)}, u32[]{:S(2)}, u32[]{:S(2)}) %collective-permute-start.5) | collective-permute-done | bytes 294944 | tf_op jit(solution)/shard_map/ppermute | solution.py:151
  131.5 6.6 %collective-permute-done.4 = bf16[2,1,72,1024]{3,2,1,0:T(8,128)(2,1)S(1)} collective-permute-done((bf16[2,1,72,1024]{3,2,1,0:T(8,128)(2,1)S(1)}, bf16[2,1,72,1024]{3,2,1,0:T(8,128)(2,1)S(1)}, u32[]{:S(2)}, u32[]{:S(2)}) %collective-permute-start.4) | collective-permute-done | bytes 294944 | tf_op jit(solution)/shard_map/ppermute | solution.py:157
  138.6 2.0 %pad_maximum_fusion.2 = bf16[2,4,72,1024]{3,1,2,0:T(4,128)(2,1)S(1)} fusion(bf16[2,1,72,1024]{3,1,2,0:T(2,128)(2,1)S(1)} %copy.42, bf16[2,2,72,1024]{3,1,2,0:T(2,128)(2,1)S(1)} %bitcast.26, bf16[2,1,72,1024]{3,1,2,0:T(2,128)(2,1)S(1)} %copy.41), kind=kLoop, calls=%fused_computation.5 | loop fusion | flops 3538944 | bytes 2359296 | tf_op jit(solution)/shard_map/concatenate | solution.py:163
  141.0 1.2 copy-done
  142.2 37.7 %shard_map.92 = bf16[2,144,1024]{2,1,0:T(8,128)(2,1)S(1)} custom-call(bf16[2,288,1024]{2,1,0:T(8,128)(2,1)S(1)} %bitcast.22, bf16[1024,3072]{1,0:T(8,128)(2,1)} %qkv_ref.3, bf16[1024,1024]{1,0:T(8,128)(2,1)S(1)} %copy-done), custom_call_target="tpu_custom_call" | custom-call | flops 7000000000 | bytes 20971520 | tf_op jit(solution)/shard_map/pallas_call | solution.py:132
  179.9 0.6 copy.44
  180.6 0.6 copy.45
  182.1 7.9 %collective-permute-done.6 = bf16[4,6,6,1024]{3,0,2,1:T(4,128)(2,1)S(1)} collective-permute-done((bf16[4,6,6,1024]{3,0,2,1:T(4,128)(2,1)S(1)}, bf16[4,6,6,1024]{3,0,2,1:T(4,128)(2,1)S(1)}, u32[]{:S(2)}, u32[]{:S(2)}) %collective-permute-start.6) | collective-permute-done | bytes 294944 | tf_op jit(solution)/shard_map/ppermute | solution.py:157
  190.0 1.2 fusion.2
  (28 shorter events, 5.6 us)
Async XLA Ops:
  1.0 8.4 %collective-permute-start = (bf16[4,12,6,512]{3,2,1,0:T(8,128)(2,1)S(1)}, bf16[4,12,6,512]{3,2,1,0:T(8,128)(2,1)S(1)}, u32[]{:S(2)}, u32[]{:S(2)}) collective-permute-start(bf16[4,12,6,512]{3,2,1,0:T(8,128)(2,1)S(1)} %slice.43), channel_id=1, source_target_pairs={{1,0},{2,1},{3,2},{4,3},{5,4},{6,5},{7,6},{0,7},{9,8},{10,9},{11,1... | collective-permute-start | bytes 884744 | tf_op jit(solution)/shard_map/ppermute | solution.py:151
  12.9 7.7 %collective-permute-start.2 = (bf16[4,1,72,512]{3,2,1,0:T(8,128)(2,1)S(1)}, bf16[4,1,72,512]{3,2,1,0:T(8,128)(2,1)S(1)}, u32[]{:S(2)}, u32[]{:S(2)}) collective-permute-start(bf16[4,1,72,512]{3,2,1,0:T(8,128)(2,1)S(1)} %copy.32), channel_id=1, source_target_pairs={{8,0},{16,8},{24,16},{9,1},{17,9},{25,17},{10,2},{18,10},{26,18},{... | collective-permute-start | bytes 884744 | tf_op jit(solution)/shard_map/ppermute | solution.py:151
  15.4 13.4 %collective-permute-start.1 = (bf16[4,1,72,512]{3,2,1,0:T(8,128)(2,1)S(1)}, bf16[4,1,72,512]{3,2,1,0:T(8,128)(2,1)S(1)}, u32[]{:S(2)}, u32[]{:S(2)}) collective-permute-start(bf16[4,1,72,512]{3,2,1,0:T(8,128)(2,1)S(1)} %copy.31), channel_id=1, source_target_pairs={{0,8},{8,16},{16,24},{1,9},{9,17},{17,25},{2,10},{10,18},{18,26},{... | collective-permute-start | bytes 884744 | tf_op jit(solution)/shard_map/ppermute | solution.py:157
  31.2 1.4 copy-start.1
  31.3 1.5 copy-start.2
  31.3 1.5 copy-start.3
  117.0 5.1 %collective-permute-start.3 = (bf16[4,6,3,1024]{3,0,2,1:T(4,128)(2,1)S(1)}, bf16[4,6,3,1024]{3,0,2,1:T(4,128)(2,1)S(1)}, u32[]{:S(2)}, u32[]{:S(2)}) collective-permute-start(bf16[4,6,3,1024]{3,0,2,1:T(4,128)(2,1)S(1)} %slice.61), channel_id=1, source_target_pairs={{1,0},{2,1},{3,2},{4,3},{5,4},{6,5},{7,6},{0,7},{9,8},{10,9},{11,1... | collective-permute-start | bytes 442376 | tf_op jit(solution)/shard_map/ppermute | solution.py:151
  124.3 6.8 %collective-permute-start.5 = (bf16[2,1,72,1024]{3,2,1,0:T(8,128)(2,1)S(1)}, bf16[2,1,72,1024]{3,2,1,0:T(8,128)(2,1)S(1)}, u32[]{:S(2)}, u32[]{:S(2)}) collective-permute-start(bf16[2,1,72,1024]{3,2,1,0:T(8,128)(2,1)S(1)} %copy.40), channel_id=1, source_target_pairs={{8,0},{16,8},{24,16},{9,1},{17,9},{25,17},{10,2},{18,10},{26,18},{... | collective-permute-start | bytes 884744 | tf_op jit(solution)/shard_map/ppermute | solution.py:151
  126.8 11.3 %collective-permute-start.4 = (bf16[2,1,72,1024]{3,2,1,0:T(8,128)(2,1)S(1)}, bf16[2,1,72,1024]{3,2,1,0:T(8,128)(2,1)S(1)}, u32[]{:S(2)}, u32[]{:S(2)}) collective-permute-start(bf16[2,1,72,1024]{3,2,1,0:T(8,128)(2,1)S(1)} %copy.39), channel_id=1, source_target_pairs={{0,8},{8,16},{16,24},{1,9},{9,17},{17,25},{2,10},{10,18},{18,26},{... | collective-permute-start | bytes 884744 | tf_op jit(solution)/shard_map/ppermute | solution.py:157
  140.6 1.6 copy-start
  182.1 8.0 %collective-permute-start.6 = (bf16[4,6,6,1024]{3,0,2,1:T(4,128)(2,1)S(1)}, bf16[4,6,6,1024]{3,0,2,1:T(4,128)(2,1)S(1)}, u32[]{:S(2)}, u32[]{:S(2)}) collective-permute-start(bf16[4,6,6,1024]{3,0,2,1:T(4,128)(2,1)S(1)} %fusion.3), channel_id=1, source_target_pairs={{0,1},{1,2},{2,3},{3,4},{4,5},{5,6},{6,7},{7,0},{8,9},{9,10},{10,1... | collective-permute-start | bytes 884744 | tf_op jit(solution)/shard_map/ppermute | solution.py:157

commit v2 on v1

--- a/solution.py
+++ b/solution.py
@@ -42,6 +42,7 @@
     top = jnp.minimum(bias, jnp.where(key < SEG, first, 0.0))
     bottom = jnp.minimum(bias, jnp.where(key >= SEG, final, 0.0))
     head_of = lax.broadcasted_iota(jnp.int32, (1, LANES), 1) // size
+    head_twice = lax.broadcasted_iota(jnp.int32, (1, 2 * LANES), 1) % LANES // size
     ones = jnp.ones((2 * SEG, LANES), BF16)
 
     def group(g, carry):
@@ -51,25 +52,26 @@
             keys = kv_ref[rows, pl.ds(lane, LANES)]
             values = kv_ref[rows, pl.ds(pl.multiple_of(chan + lane, LANES), LANES)]
             values = jnp.concatenate([values, ones], 1)
-            for s in (2 * w - 1, 2 * w):
-                if s < 0 or s >= segs:
-                    continue
-                shut = top if w == 0 else bottom if w == windows - 1 else bias
-                mine = pl.ds(s * SEG, SEG)
-                q = q_ref[mine, pl.ds(lane, LANES)]
-                total = jnp.zeros((SEG, LANES), F32)
-                for h in range(per):
-                    q_h = jnp.where(head_of == h, q, 0.0).astype(BF16)
-                    scores = lax.dot_general(
-                        q_h, keys, (((1,), (1,)), ((), ())), preferred_element_type=F32
-                    ) + shut
-                    expo = jnp.exp(scores - jnp.max(scores, -1, keepdims=True)).astype(BF16)
-                    both = matmul(expo, values)
-                    total = jnp.where(head_of == h, both[:, :LANES] / both[:, LANES:], total)
-                out_ref[mine, pl.ds(lane, LANES)] = total
+            segments = [s for s in (2 * w - 1, 2 * w) if 0 <= s < segs]
+            shut = top if w == 0 else bottom if w == windows - 1 else bias
+            count = len(segments) * SEG
+            mine = pl.ds(segments[0] * SEG, count)
+            q = q_ref[mine, pl.ds(lane, LANES)]
+            stacked = jnp.concatenate([jnp.where(head_of == h, q, 0.0) for h in range(per)], 0)
+            scores = lax.dot_general(
+                stacked.astype(BF16), keys, (((1,), (1,)), ((), ())), preferred_element_type=F32
+            )
+            scores = scores.reshape(per * len(segments), SEG, 2 * SEG) + shut[None]
+            expo = jnp.exp(scores - jnp.max(scores, -1, keepdims=True))
+            both = matmul(expo.reshape(per * count, 2 * SEG).astype(BF16), values)
+            total = both[:count]
+            for h in range(1, per):
+                part = both[h * count : (h + 1) * count]
+                total = jnp.where(head_twice == h, part, total)
+            out_ref[mine, pl.ds(lane, LANES)] = total[:, :LANES] / total[:, LANES:]
         return carry
 
-    lax.fori_loop(0, chan // LANES, group, 0)
+    lax.fori_loop(0, chan // LANES, group, 0, unroll=2)
 
 
 def project(x, w_ref, q_ref, kv_ref, heads, chan):
@@ -81,16 +83,17 @@
     )
 
 
-def fine_kernel(col_win, x_ref, qkv_ref, out_ref, up_ref, down_ref, merge_ref, pick_ref, merged_ref,
+def fine_kernel(col_win, low_ref, x_ref, high_ref, qkv_ref, out_ref, up_ref, down_ref, merge_ref, pick_ref, merged_ref,
                 q_ref, kv_ref, att_ref):
     lat, last = lax.axis_index("lat"), lax.axis_size("lat") - 1
     own, chan = q_ref.shape
     x = x_ref[0].astype(F32)
-    project(x, qkv_ref, q_ref, kv_ref, HEADS, chan)
+    wide = [low_ref[0].astype(F32), x, high_ref[0].astype(F32)]
+    project(jnp.concatenate(wide, 0), qkv_ref, q_ref, kv_ref, HEADS, chan)
     pair = pl.program_id(0) // col_win
     attend(q_ref, kv_ref, att_ref, pair, lat, last, own // SEG, HEADS, chan)
     mixed = matmul(att_ref[...].astype(BF16), out_ref[...])
-    hidden = (x[SEG : SEG + own] + mixed).astype(BF16).astype(F32)
+    hidden = (x + mixed).astype(BF16).astype(F32)
     second = normalize(hidden).astype(BF16)
     block = hidden
     width = up_ref.shape[1]
@@ -113,26 +116,32 @@
     merged_ref[0] = merged.astype(BF16)
 
 
-def coarse_kernel(x_ref, qkv_ref, out_ref, res_ref, q_ref, kv_ref, att_ref):
+def coarse_kernel(low_ref, x_ref, high_ref, qkv_ref, out_ref, res_ref, q_ref, kv_ref, att_ref):
     lat, last = lax.axis_index("lat"), lax.axis_size("lat") - 1
     own, chan = q_ref.shape
     x = x_ref[0].astype(F32)
-    project(x, qkv_ref, q_ref, kv_ref, HEADS2, chan)
+    wide = [low_ref[0].astype(F32), x, high_ref[0].astype(F32)]
+    project(jnp.concatenate(wide, 0), qkv_ref, q_ref, kv_ref, HEADS2, chan)
     attend(q_ref, kv_ref, att_ref, pl.program_id(0), lat, last, own // SEG, HEADS2, chan)
     mixed = matmul(att_ref[...].astype(BF16), out_ref[...])
-    res_ref[0] = (x[SEG : SEG + own] + mixed).astype(BF16)
-
-
-def call(kernel, ext, weights, out_rows, out_width, chan, flops):
-    steps, rows, width = ext.shape
-    own = rows - 2 * SEG
+    res_ref[0] = (x + mixed).astype(BF16)
+
+
+def call(kernel, segments, weights, out_rows, out_width, chan, flops):
+    low = from_last(segments[:, -1], "lat", False)
+    high = from_next(segments[:, 0], "lat", False)
+    steps, segs, _, width = segments.shape
+    own = segs * SEG
+    rows = own + 2 * SEG
+    tokens = [low, segments.reshape(steps, own, width), high]
+    pieces = [pl.BlockSpec((1,) + t.shape[1:], lambda i: (i, 0, 0)) for t in tokens]
     whole = [
         pl.BlockSpec(w.shape, lambda i: (0, 0), pipeline_mode=pl.Buffered(1)) for w in weights
     ]
     return pl.pallas_call(
         kernel,
         grid=(steps,),
-        in_specs=[pl.BlockSpec((1, rows, width), lambda i: (i, 0, 0))] + whole,
+        in_specs=pieces + whole,
         out_specs=pl.BlockSpec((1, out_rows, out_width), lambda i: (i, 0, 0)),
         out_shape=jax.ShapeDtypeStruct((steps, out_rows, out_width), BF16),
         scratch_shapes=[
@@ -142,7 +151,7 @@
         ],
         compiler_params=pltpu.CompilerParams(vmem_limit_bytes=48 * 2**20),
         cost_estimate=pl.CostEstimate(flops=flops, bytes_accessed=20 * 2**20, transcendentals=0),
-    )(ext, *weights)
+    )(*tokens, *weights)
 
 
 def from_next(block, axis, periodic):
@@ -155,13 +164,6 @@
     count = lax.axis_size(axis)
     pairs = [(i, i + 1) for i in range(count - 1)] + ([(count - 1, 0)] if periodic else [])
     return lax.ppermute(block, axis, pairs)
-
-
-def widen(segments):
-    low = from_last(segments[:, -1:], "lat", False)
-    high = from_next(segments[:, :1], "lat", False)
-    ext = jnp.concatenate([low, segments, high], 1)
-    return ext.reshape(ext.shape[0], -1, ext.shape[-1])
 
 
 def pick_matrix(rows):
@@ -186,7 +188,7 @@
     pick = jnp.asarray(pick_matrix(rows), BF16)
     wide = merge_weight.shape[1]
     merged = call(
-        functools.partial(fine_kernel, col_win), widen(segments),
+        functools.partial(fine_kernel, col_win), segments,
         (fine_qkv, fine_out, fine_up, fine_down, merge_weight, pick),
         rows * COLS // 2, wide, chan, 14 * 10**9,
     )
@@ -198,7 +200,7 @@
     split = merged.reshape(2, 2, rows2 // ROWS, ROWS, win2, COLS, wide)
     segments = split.transpose(0, 4, 2, 1, 3, 5, 6).reshape(2 * win2, rows2 // ROWS, SEG, wide)
     coarse = call(
-        coarse_kernel, widen(segments), (coarse_qkv, coarse_out),
+        coarse_kernel, segments, (coarse_qkv, coarse_out),
         rows2 * 2 * COLS, wide, wide, 7 * 10**9,
     )
     coarse = coarse.reshape(2, win2, rows2 // ROWS, 2, ROWS, COLS, wide)

time: 192 us -> 115 us (0.60)
  the two profiles are of different devices: /device:TPU:6 before, /device:TPU:0 now
where the time goes in v2:
time: 115 us; the launch traced here: 114 us
  Pallas kernels  46 us (40%)
  waiting for transfers between devices  31.1 us (27%)
  local copies, waits for them, and re-layouts  17.4 us (15%)
  starting transfers between devices  17.3 us (15%)
  other arithmetic  2.24 us (2%)
    pallas_call x2, Pallas kernels, call(): pl.pallas_call(kernel, grid=(steps,), in_specs=pieces + whole, out_specs=...  46 us
    ppermute x4, waiting for transfers between devices, from_next(): return lax.ppermute(block, axis, pairs)  20.9 us
    ppermute x3, waiting for transfers between devices, from_last(): return lax.ppermute(block, axis, pairs)  10.2 us
    ppermute x4, starting transfers between devices, from_next(): return lax.ppermute(block, axis, pairs)  9.62 us
    ppermute x3, starting transfers between devices, from_last(): return lax.ppermute(block, axis, pairs)  7.64 us
    another operation x3, local copies, waits for them, and re-layouts, call(): tokens = [low, segments.reshape(steps, own, width), high]  4.05 us
  transfers between devices with their start and end apart: 7, of which 6 were waited for; matrix products, arithmetic and copies ran while one was open for 6% of the time, Pallas kernels for 0%

profile of v2, /device:TPU:0, one launch (start us, length us, event | category | flops | bytes accessed | tf_op | source)
XLA Modules:
  0.0 114.3 jit_solution(4229168295812580783)
XLA Ops:
  0.0 1.0 slice.43
  1.0 4.5 %collective-permute-start = (bf16[4,12,6,512]{3,2,1,0:T(8,128)(2,1)S(1)}, bf16[4,12,6,512]{3,2,1,0:T(8,128)(2,1)S(1)}, u32[]{:S(2)}, u32[]{:S(2)}) collective-permute-start(bf16[4,12,6,512]{3,2,1,0:T(8,128)(2,1)S(1)} %slice.43), channel_id=1, source_target_pairs={{1,0},{2,1},{3,2},{4,3},{5,4},{6,5},{7,6},{0,7},{9,8},{10,9},{11,1... | collective-permute-start | bytes 884744 | tf_op jit(solution)/shard_map/ppermute | solution.py:160
  5.6 1.8 %slice.42 = bf16[4,12,18,512]{3,2,1,0:T(8,128)(2,1)S(1)} slice(bf16[4,12,24,512]{3,2,1,0:T(8,128)(2,1)} %param.9), slice={[0:4], [0:12], [6:24], [0:512]} | slice | bytes 1769472 | tf_op jit(solution)/shard_map/slice | solution.py:184
  7.4 3.5 %collective-permute-done = bf16[4,12,6,512]{3,2,1,0:T(8,128)(2,1)S(1)} collective-permute-done((bf16[4,12,6,512]{3,2,1,0:T(8,128)(2,1)S(1)}, bf16[4,12,6,512]{3,2,1,0:T(8,128)(2,1)S(1)}, u32[]{:S(2)}, u32[]{:S(2)}) %collective-permute-start) | collective-permute-done | bytes 294944 | tf_op jit(solution)/shard_map/ppermute | solution.py:160
  11.2 0.9 copy.28
  12.1 0.5 reshape.24
  12.6 0.9 copy.29
  13.5 0.8 fusion.4
  14.3 0.8 copy.55
  15.1 0.8 copy.56
  15.9 4.1 %collective-permute-start.1 = (bf16[4,72,512]{2,1,0:T(8,128)(2,1)}, bf16[4,72,512]{2,1,0:T(8,128)(2,1)}, u32[]{:S(2)}, u32[]{:S(2)}) collective-permute-start(bf16[4,72,512]{2,1,0:T(8,128)(2,1)} %bitcast.30), channel_id=1, source_target_pairs={{0,8},{8,16},{16,24},{1,9},{9,17},{17,25},{2,10},{10,18},{18,26},{... | collective-permute-start | bytes 884744 | tf_op jit(solution)/shard_map/ppermute | solution.py:166
  20.0 1.3 %collective-permute-start.2 = (bf16[4,72,512]{2,1,0:T(8,128)(2,1)}, bf16[4,72,512]{2,1,0:T(8,128)(2,1)}, u32[]{:S(2)}, u32[]{:S(2)}) collective-permute-start(bf16[4,72,512]{2,1,0:T(8,128)(2,1)} %bitcast.29), channel_id=1, source_target_pairs={{8,0},{16,8},{24,16},{9,1},{17,9},{25,17},{10,2},{18,10},{26,18},{... | collective-permute-start | bytes 884744 | tf_op jit(solution)/shard_map/ppermute | solution.py:160
  21.3 1.5 %copy.43 = bf16[2,2,4,2,3,12,512]{6,5,4,3,2,1,0:T(8,128)(2,1)} copy(bf16[2,2,4,2,3,12,512]{6,3,0,5,1,4,2:T(2,128)(2,1)S(1)} %bitcast.33) | data formatting | bytes 2359296 | tf_op jit(solution)/shard_map/reshape;reshape | solution.py:136
  22.8 2.4 %reshape.32.x_ref = bf16[4,288,512]{2,1,0:T(8,128)(2,1)S(1)} reshape(bf16[2,2,4,2,3,12,512]{6,5,4,3,2,1,0:T(8,128)(2,1)} %copy.43) | data formatting | bytes 2359296 | tf_op jit(solution)/shard_map/reshape;reshape | solution.py:136
  25.2 7.8 %collective-permute-done.2.high_ref = bf16[4,72,512]{2,1,0:T(8,128)(2,1)} collective-permute-done((bf16[4,72,512]{2,1,0:T(8,128)(2,1)}, bf16[4,72,512]{2,1,0:T(8,128)(2,1)}, u32[]{:S(2)}, u32[]{:S(2)}) %collective-permute-start.2) | collective-permute-done | bytes 294944 | tf_op jit(solution)/shard_map/ppermute | solution.py:160
  33.1 31.3 %shard_map.91 = bf16[4,72,1024]{2,1,0:T(8,128)(2,1)S(1)} custom-call(bf16[4,72,512]{2,1,0:T(8,128)(2,1)} %collective-permute-done.1.low_ref, bf16[4,288,512]{2,1,0:T(8,128)(2,1)S(1)} %reshape.32.x_ref, bf16[4,72,512]{2,1,0:T(8,128)(2,1)} %collective-permute-done.2.high_ref, bf16[512,1536]{1,0:T(8,128)(2,1)S(1)} %copy-done.1, bf16[512,512]{1,0:T(8,128)(2,1)S(1)} %copy-done.2, ...), custom_call_target="tpu_custom_call" | custom-call | flops 14000000000 | bytes 20971520 | tf_op jit(solution)/shard_map/pallas_call | solution.py:141
  64.4 0.5 copy.34
  65.1 0.6 copy.35
  66.0 2.4 %collective-permute-start.3 = (bf16[4,6,3,1024]{3,0,2,1:T(4,128)(2,1)S(1)}, bf16[4,6,3,1024]{3,0,2,1:T(4,128)(2,1)S(1)}, u32[]{:S(2)}, u32[]{:S(2)}) collective-permute-start(bf16[4,6,3,1024]{3,0,2,1:T(4,128)(2,1)S(1)} %slice.61), channel_id=1, source_target_pairs={{1,0},{2,1},{3,2},{4,3},{5,4},{6,5},{7,6},{0,7},{9,8},{10,9},{11,1... | collective-permute-start | bytes 442376 | tf_op jit(solution)/shard_map/ppermute | solution.py:160
  68.5 2.5 %collective-permute-done.3 = bf16[4,6,3,1024]{3,0,2,1:T(4,128)(2,1)S(1)} collective-permute-done((bf16[4,6,3,1024]{3,0,2,1:T(4,128)(2,1)S(1)}, bf16[4,6,3,1024]{3,0,2,1:T(4,128)(2,1)S(1)}, u32[]{:S(2)}, u32[]{:S(2)}) %collective-permute-start.3) | collective-permute-done | bytes 147488 | tf_op jit(solution)/shard_map/ppermute | solution.py:160
  71.6 0.6 copy.36
  72.3 0.8 fusion.5
  73.3 3.5 %collective-permute-start.4 = (bf16[2,72,1024]{2,1,0:T(8,128)(2,1)S(1)}, bf16[2,72,1024]{2,1,0:T(8,128)(2,1)S(1)}, u32[]{:S(2)}, u32[]{:S(2)}) collective-permute-start(bf16[2,72,1024]{2,1,0:T(8,128)(2,1)S(1)} %bitcast.44), channel_id=1, source_target_pairs={{0,8},{8,16},{16,24},{1,9},{9,17},{17,25},{2,10},{10,18},{18,26},{... | collective-permute-start | bytes 884744 | tf_op jit(solution)/shard_map/ppermute | solution.py:166
  76.8 1.4 %collective-permute-start.5 = (bf16[2,72,1024]{2,1,0:T(8,128)(2,1)S(1)}, bf16[2,72,1024]{2,1,0:T(8,128)(2,1)S(1)}, u32[]{:S(2)}, u32[]{:S(2)}) collective-permute-start(bf16[2,72,1024]{2,1,0:T(8,128)(2,1)S(1)} %bitcast.43), channel_id=1, source_target_pairs={{8,0},{16,8},{24,16},{9,1},{17,9},{25,17},{10,2},{18,10},{26,18},{... | collective-permute-start | bytes 884744 | tf_op jit(solution)/shard_map/ppermute | solution.py:160
  78.2 0.5 copy.38
  78.8 2.3 %collective-permute-done.4.low_ref = bf16[2,72,1024]{2,1,0:T(8,128)(2,1)S(1)} collective-permute-done((bf16[2,72,1024]{2,1,0:T(8,128)(2,1)S(1)}, bf16[2,72,1024]{2,1,0:T(8,128)(2,1)S(1)}, u32[]{:S(2)}, u32[]{:S(2)}) %collective-permute-start.4) | collective-permute-done | bytes 294944 | tf_op jit(solution)/shard_map/ppermute | solution.py:166
  81.1 7.1 %collective-permute-done.5.high_ref = bf16[2,72,1024]{2,1,0:T(8,128)(2,1)S(1)} collective-permute-done((bf16[2,72,1024]{2,1,0:T(8,128)(2,1)S(1)}, bf16[2,72,1024]{2,1,0:T(8,128)(2,1)S(1)}, u32[]{:S(2)}, u32[]{:S(2)}) %collective-permute-start.5) | collective-permute-done | bytes 294944 | tf_op jit(solution)/shard_map/ppermute | solution.py:160
  88.2 14.8 %shard_map.92 = bf16[2,144,1024]{2,1,0:T(8,128)(2,1)S(1)} custom-call(bf16[2,72,1024]{2,1,0:T(8,128)(2,1)S(1)} %collective-permute-done.4.low_ref, bf16[2,144,1024]{2,1,0:T(8,128)(2,1)S(1)} %copy.40.x_ref, bf16[2,72,1024]{2,1,0:T(8,128)(2,1)S(1)} %collective-permute-done.5.high_ref, bf16[1024,3072]{1,0:T(8,128)(2,1)} %qkv_ref.3, bf16[1024,1024]{1,0:T(8,128)(2,1)S(1)} %copy-done), custom_call_target="tpu_custom_call" | custom-call | flops 7000000000 | bytes 20971520 | tf_op jit(solution)/shard_map/pallas_call | solution.py:141
  103.0 0.6 copy.41
  103.6 0.6 copy.42
  105.1 7.9 %collective-permute-done.6 = bf16[4,6,6,1024]{3,0,2,1:T(4,128)(2,1)S(1)} collective-permute-done((bf16[4,6,6,1024]{3,0,2,1:T(4,128)(2,1)S(1)}, bf16[4,6,6,1024]{3,0,2,1:T(4,128)(2,1)S(1)}, u32[]{:S(2)}, u32[]{:S(2)}) %collective-permute-start.6) | collective-permute-done | bytes 294944 | tf_op jit(solution)/shard_map/ppermute | solution.py:166
  113.1 1.2 %fusion.2 = bf16[4,6,12,1024]{3,0,2,1:T(4,128)(2,1)} fusion(bf16[3,6,12,1024]{3,0,2,1:T(4,128)(2,1)S(1)} %bitcast.35, bf16[1,6,12,1024]{3,0,2,1:T(2,128)(2,1)S(1)} %slice.64, bf16[4,6,6,1024]{3,0,2,1:T(4,128)(2,1)S(1)} %collective-permute-done.6), kind=kLoop, calls=%fused_computation.6 | loop fusion | flops 1769472 | bytes 1474560 | tf_op jit(solution)/shard_map/concatenate | solution.py:210
  (24 shorter events, 2.8 us)
Async XLA Ops:
  1.0 9.8 %collective-permute-start = (bf16[4,12,6,512]{3,2,1,0:T(8,128)(2,1)S(1)}, bf16[4,12,6,512]{3,2,1,0:T(8,128)(2,1)S(1)}, u32[]{:S(2)}, u32[]{:S(2)}) collective-permute-start(bf16[4,12,6,512]{3,2,1,0:T(8,128)(2,1)S(1)} %slice.43), channel_id=1, source_target_pairs={{1,0},{2,1},{3,2},{4,3},{5,4},{6,5},{7,6},{0,7},{9,8},{10,9},{11,1... | collective-permute-start | bytes 884744 | tf_op jit(solution)/shard_map/ppermute | solution.py:160
  15.9 9.4 %collective-permute-start.1 = (bf16[4,72,512]{2,1,0:T(8,128)(2,1)}, bf16[4,72,512]{2,1,0:T(8,128)(2,1)}, u32[]{:S(2)}, u32[]{:S(2)}) collective-permute-start(bf16[4,72,512]{2,1,0:T(8,128)(2,1)} %bitcast.30), channel_id=1, source_target_pairs={{0,8},{8,16},{16,24},{1,9},{9,17},{17,25},{2,10},{10,18},{18,26},{... | collective-permute-start | bytes 884744 | tf_op jit(solution)/shard_map/ppermute | solution.py:166
  20.0 13.1 %collective-permute-start.2 = (bf16[4,72,512]{2,1,0:T(8,128)(2,1)}, bf16[4,72,512]{2,1,0:T(8,128)(2,1)}, u32[]{:S(2)}, u32[]{:S(2)}) collective-permute-start(bf16[4,72,512]{2,1,0:T(8,128)(2,1)} %bitcast.29), channel_id=1, source_target_pairs={{8,0},{16,8},{24,16},{9,1},{17,9},{25,17},{10,2},{18,10},{26,18},{... | collective-permute-start | bytes 884744 | tf_op jit(solution)/shard_map/ppermute | solution.py:160
  22.8 10.3 %copy-start.1 = (bf16[512,1536]{1,0:T(8,128)(2,1)S(1)}, bf16[512,1536]{1,0:T(8,128)(2,1)}, u32[]{:S(2)}) copy-start(bf16[512,1536]{1,0:T(8,128)(2,1)} %qkv_ref.2) | copy-start | bytes 4718596
  22.8 10.3 %copy-start.2 = (bf16[512,512]{1,0:T(8,128)(2,1)S(1)}, bf16[512,512]{1,0:T(8,128)(2,1)}, u32[]{:S(2)}) copy-start(bf16[512,512]{1,0:T(8,128)(2,1)} %out_ref.2) | copy-start | bytes 1572868
  22.8 10.3 %copy-start.3 = (bf16[288,288]{1,0:T(8,128)(2,1)S(1)}, bf16[288,288]{1,0:T(8,128)(2,1)}, u32[]{:S(2)}) copy-start(bf16[288,288]{1,0:T(8,128)(2,1)} %constant.2.clone.pick_ref) | copy-start | bytes 497668
  66.0 5.1 %collective-permute-start.3 = (bf16[4,6,3,1024]{3,0,2,1:T(4,128)(2,1)S(1)}, bf16[4,6,3,1024]{3,0,2,1:T(4,128)(2,1)S(1)}, u32[]{:S(2)}, u32[]{:S(2)}) collective-permute-start(bf16[4,6,3,1024]{3,0,2,1:T(4,128)(2,1)S(1)} %slice.61), channel_id=1, source_target_pairs={{1,0},{2,1},{3,2},{4,3},{5,4},{6,5},{7,6},{0,7},{9,8},{10,9},{11,1... | collective-permute-start | bytes 442376 | tf_op jit(solution)/shard_map/ppermute | solution.py:160
  73.3 7.8 %collective-permute-start.4 = (bf16[2,72,1024]{2,1,0:T(8,128)(2,1)S(1)}, bf16[2,72,1024]{2,1,0:T(8,128)(2,1)S(1)}, u32[]{:S(2)}, u32[]{:S(2)}) collective-permute-start(bf16[2,72,1024]{2,1,0:T(8,128)(2,1)S(1)} %bitcast.44), channel_id=1, source_target_pairs={{0,8},{8,16},{16,24},{1,9},{9,17},{17,25},{2,10},{10,18},{18,26},{... | collective-permute-start | bytes 884744 | tf_op jit(solution)/shard_map/ppermute | solution.py:166
  76.8 11.4 %copy-start = (bf16[1024,1024]{1,0:T(8,128)(2,1)S(1)}, bf16[1024,1024]{1,0:T(8,128)(2,1)}, u32[]{:S(2)}) copy-start(bf16[1024,1024]{1,0:T(8,128)(2,1)} %out_ref.3) | copy-start | bytes 6291460
  76.8 11.4 %collective-permute-start.5 = (bf16[2,72,1024]{2,1,0:T(8,128)(2,1)S(1)}, bf16[2,72,1024]{2,1,0:T(8,128)(2,1)S(1)}, u32[]{:S(2)}, u32[]{:S(2)}) collective-permute-start(bf16[2,72,1024]{2,1,0:T(8,128)(2,1)S(1)} %bitcast.43), channel_id=1, source_target_pairs={{8,0},{16,8},{24,16},{9,1},{17,9},{25,17},{10,2},{18,10},{26,18},{... | collective-permute-start | bytes 884744 | tf_op jit(solution)/shard_map/ppermute | solution.py:160
  105.1 8.0 %collective-permute-start.6 = (bf16[4,6,6,1024]{3,0,2,1:T(4,128)(2,1)S(1)}, bf16[4,6,6,1024]{3,0,2,1:T(4,128)(2,1)S(1)}, u32[]{:S(2)}, u32[]{:S(2)}) collective-permute-start(bf16[4,6,6,1024]{3,0,2,1:T(4,128)(2,1)S(1)} %fusion.3), channel_id=1, source_target_pairs={{0,1},{1,2},{2,3},{3,4},{4,5},{5,6},{6,7},{7,0},{8,9},{9,10},{10,1... | collective-permute-start | bytes 884744 | tf_op jit(solution)/shard_map/ppermute | solution.py:166

commit v3 on v2

--- a/solution.py
+++ b/solution.py
@@ -29,7 +29,7 @@
     return jnp.dot(a, b, preferred_element_type=F32)
 
 
-def attend(q_ref, kv_ref, out_ref, pair, lat, last, segs, heads, chan):
+def attend(q_ref, kv_ref, out_ref, pair, lat, last, segs, heads, chan, chosen):
     size = chan // heads
     per = LANES // size
     windows = (segs + 2) // 2
@@ -47,11 +47,11 @@
 
     def group(g, carry):
         lane = pl.multiple_of(g * LANES, LANES)
-        for w in range(windows):
+        for w in chosen:
             rows = pl.ds(2 * w * SEG, 2 * SEG)
-            keys = kv_ref[rows, pl.ds(lane, LANES)]
+            keys = kv_ref[rows, pl.ds(lane, LANES)].astype(BF16)
             values = kv_ref[rows, pl.ds(pl.multiple_of(chan + lane, LANES), LANES)]
-            values = jnp.concatenate([values, ones], 1)
+            values = jnp.concatenate([values.astype(BF16), ones], 1)
             segments = [s for s in (2 * w - 1, 2 * w) if 0 <= s < segs]
             shut = top if w == 0 else bottom if w == windows - 1 else bias
             count = len(segments) * SEG
@@ -62,7 +62,7 @@
                 stacked.astype(BF16), keys, (((1,), (1,)), ((), ())), preferred_element_type=F32
             )
             scores = scores.reshape(per * len(segments), SEG, 2 * SEG) + shut[None]
-            expo = jnp.exp(scores - jnp.max(scores, -1, keepdims=True))
+            expo = jnp.exp2(scores - jnp.max(scores, -1, keepdims=True))
             both = matmul(expo.reshape(per * count, 2 * SEG).astype(BF16), values)
             total = both[:count]
             for h in range(1, per):
@@ -74,24 +74,95 @@
     lax.fori_loop(0, chan // LANES, group, 0, unroll=2)
 
 
-def project(x, w_ref, q_ref, kv_ref, heads, chan):
-    own = q_ref.shape[0]
-    normed = normalize(x)
-    kv_ref[...] = matmul(normed.astype(BF16), w_ref[:, chan:]).astype(BF16)
-    q_ref[...] = matmul(normed[SEG : SEG + own].astype(BF16), w_ref[:, :chan]) * (
-        (chan // heads) ** -0.5
-    )
-
-
-def fine_kernel(col_win, low_ref, x_ref, high_ref, qkv_ref, out_ref, up_ref, down_ref, merge_ref, pick_ref, merged_ref,
-                q_ref, kv_ref, att_ref):
+def links(x_ref, halo_ref, send_sem, recv_sem, i, lat):
+    segs = x_ref.shape[1]
+
+    def copy(seg, side, device):
+        return pltpu.make_async_remote_copy(
+            src_ref=x_ref.at[i, seg], dst_ref=halo_ref.at[i, side],
+            send_sem=send_sem.at[i, side], recv_sem=recv_sem.at[i, side],
+            device_id={"lat": device}, device_id_type=pl.DeviceIdType.MESH,
+        )
+
+    return copy(segs - 1, 0, lat + 1), copy(0, 1, lat - 1)
+
+
+def attention(x_ref, w_ref, q_ref, kv_ref, att_ref, halo_ref, send_sem, recv_sem, pair, heads):
     lat, last = lax.axis_index("lat"), lax.axis_size("lat") - 1
+    step = pl.program_id(0)
+    steps, segs, _, chan = x_ref.shape
+    own = segs * SEG
+
+    @pl.when(step == 0)
+    def _():
+        barrier = pltpu.get_barrier_semaphore()
+
+        @pl.when(lat > 0)
+        def _():
+            pl.semaphore_signal(
+                barrier, inc=1, device_id={"lat": lat - 1}, device_id_type=pl.DeviceIdType.MESH
+            )
+
+        @pl.when(lat < last)
+        def _():
+            pl.semaphore_signal(
+                barrier, inc=1, device_id={"lat": lat + 1}, device_id_type=pl.DeviceIdType.MESH
+            )
+
+        @pl.when((lat > 0) & (lat < last))
+        def _():
+            pl.semaphore_wait(barrier, 2)
+
+        @pl.when((lat == 0) | (lat == last))
+        def _():
+            pl.semaphore_wait(barrier, 1)
+
+        for i in range(steps):
+            down, up = links(x_ref, halo_ref, send_sem, recv_sem, i, lat)
+            pl.when(lat < last)(down.start)
+            pl.when(lat > 0)(up.start)
+
+        @pl.when(lat == 0)
+        def _():
+            halo_ref[:, 0] = jnp.zeros((steps, SEG, chan), BF16)
+
+        @pl.when(lat == last)
+        def _():
+            halo_ref[:, 1] = jnp.zeros((steps, SEG, chan), BF16)
+
+    x = jnp.concatenate([x_ref[step, s].astype(F32) for s in range(segs)], 0)
+    normed = normalize(x).astype(BF16)
+    scale = (chan // heads) ** -0.5 * np.log2(np.e)
+    q_ref[...] = matmul(normed, w_ref[:, :chan]) * np.float32(scale)
+    kv_ref[SEG : SEG + own] = matmul(normed, w_ref[:, chan:])
+    windows = (segs + 2) // 2
+    inside = list(range(1, windows - 1))
+    if inside:
+        attend(q_ref, kv_ref, att_ref, pair, lat, last, segs, heads, chan, inside)
+    down, up = links(x_ref, halo_ref, send_sem, recv_sem, step, lat)
+    pl.when(lat > 0)(down.wait_recv)
+    pl.when(lat < last)(up.wait_recv)
+    halo = jnp.concatenate([halo_ref[step, 0].astype(F32), halo_ref[step, 1].astype(F32)], 0)
+    halo = matmul(normalize(halo).astype(BF16), w_ref[:, chan:])
+    kv_ref[:SEG] = halo[:SEG]
+    kv_ref[SEG + own :] = halo[SEG:]
+    attend(q_ref, kv_ref, att_ref, pair, lat, last, segs, heads, chan, [0, windows - 1])
+
+    @pl.when(step == steps - 1)
+    def _():
+        for i in range(steps):
+            down, up = links(x_ref, halo_ref, send_sem, recv_sem, i, lat)
+            pl.when(lat < last)(down.wait_send)
+            pl.when(lat > 0)(up.wait_send)
+
+    return x
+
+
+def fine_kernel(col_win, x_ref, qkv_ref, out_ref, up_ref, down_ref, merge_ref, pick_ref, merged_ref,
+                q_ref, kv_ref, att_ref, halo_ref, send_sem, recv_sem):
     own, chan = q_ref.shape
-    x = x_ref[0].astype(F32)
-    wide = [low_ref[0].astype(F32), x, high_ref[0].astype(F32)]
-    project(jnp.concatenate(wide, 0), qkv_ref, q_ref, kv_ref, HEADS, chan)
-    pair = pl.program_id(0) // col_win
-    attend(q_ref, kv_ref, att_ref, pair, lat, last, own // SEG, HEADS, chan)
+    x = attention(x_ref, qkv_ref, q_ref, kv_ref, att_ref, halo_ref, send_sem, recv_sem,
+                  pl.program_id(0) // col_win, HEADS)
     mixed = matmul(att_ref[...].astype(BF16), out_ref[...])
     hidden = (x + mixed).astype(BF16).astype(F32)
     second = normalize(hidden).astype(BF16)
@@ -116,42 +187,41 @@
     merged_ref[0] = merged.astype(BF16)
 
 
-def coarse_kernel(low_ref, x_ref, high_ref, qkv_ref, out_ref, res_ref, q_ref, kv_ref, att_ref):
-    lat, last = lax.axis_index("lat"), lax.axis_size("lat") - 1
-    own, chan = q_ref.shape
-    x = x_ref[0].astype(F32)
-    wide = [low_ref[0].astype(F32), x, high_ref[0].astype(F32)]
-    project(jnp.concatenate(wide, 0), qkv_ref, q_ref, kv_ref, HEADS2, chan)
-    attend(q_ref, kv_ref, att_ref, pl.program_id(0), lat, last, own // SEG, HEADS2, chan)
+def coarse_kernel(win, x_ref, qkv_ref, out_ref, res_ref,
+                  q_ref, kv_ref, att_ref, halo_ref, send_sem, recv_sem):
+    x = attention(x_ref, qkv_ref, q_ref, kv_ref, att_ref, halo_ref, send_sem, recv_sem,
+                  pl.program_id(0) // win, HEADS2)
     mixed = matmul(att_ref[...].astype(BF16), out_ref[...])
     res_ref[0] = (x + mixed).astype(BF16)
 
 
-def call(kernel, segments, weights, out_rows, out_width, chan, flops):
-    low = from_last(segments[:, -1], "lat", False)
-    high = from_next(segments[:, 0], "lat", False)
+def call(kernel, segments, weights, out_rows, out_width, chan, flops, ident):
     steps, segs, _, width = segments.shape
     own = segs * SEG
     rows = own + 2 * SEG
-    tokens = [low, segments.reshape(steps, own, width), high]
-    pieces = [pl.BlockSpec((1,) + t.shape[1:], lambda i: (i, 0, 0)) for t in tokens]
+    tokens = pl.BlockSpec(segments.shape, lambda i: (0, 0, 0, 0), pipeline_mode=pl.Buffered(1))
     whole = [
         pl.BlockSpec(w.shape, lambda i: (0, 0), pipeline_mode=pl.Buffered(1)) for w in weights
     ]
     return pl.pallas_call(
         kernel,
         grid=(steps,),
-        in_specs=pieces + whole,
+        in_specs=[tokens] + whole,
         out_specs=pl.BlockSpec((1, out_rows, out_width), lambda i: (i, 0, 0)),
         out_shape=jax.ShapeDtypeStruct((steps, out_rows, out_width), BF16),
         scratch_shapes=[
             pltpu.VMEM((own, chan), F32),
-            pltpu.VMEM((rows, 2 * chan), BF16),
+            pltpu.VMEM((rows, 2 * chan), F32),
             pltpu.VMEM((own, chan), F32),
+            pltpu.VMEM((steps, 2, SEG, width), BF16),
+            pltpu.SemaphoreType.DMA((steps, 2)),
+            pltpu.SemaphoreType.DMA((steps, 2)),
         ],
-        compiler_params=pltpu.CompilerParams(vmem_limit_bytes=48 * 2**20),
+        compiler_params=pltpu.CompilerParams(
+            vmem_limit_bytes=36 * 2**20, collective_id=ident, has_side_effects=True
+        ),
         cost_estimate=pl.CostEstimate(flops=flops, bytes_accessed=20 * 2**20, transcendentals=0),
-    )(*tokens, *weights)
+    )(segments, *weights)
 
 
 def from_next(block, axis, periodic):
@@ -190,7 +260,7 @@
     merged = call(
         functools.partial(fine_kernel, col_win), segments,
         (fine_qkv, fine_out, fine_up, fine_down, merge_weight, pick),
-        rows * COLS // 2, wide, chan, 14 * 10**9,
+        rows * COLS // 2, wide, chan, 14 * 10**9, 0,
     )
     rows2, cols2 = rows // 2, cols // 2
     merged = merged.reshape(2, col_win, 2, rows2, COLS // 2, wide).transpose(0, 2, 3, 1, 4, 5)
@@ -200,8 +270,8 @@
     split = merged.reshape(2, 2, rows2 // ROWS, ROWS, win2, COLS, wide)
     segments = split.transpose(0, 4, 2, 1, 3, 5, 6).reshape(2 * win2, rows2 // ROWS, SEG, wide)
     coarse = call(
-        coarse_kernel, segments, (coarse_qkv, coarse_out),
-        rows2 * 2 * COLS, wide, wide, 7 * 10**9,
+        functools.partial(coarse_kernel, win2), segments, (coarse_qkv, coarse_out),
+        rows2 * 2 * COLS, wide, wide, 7 * 10**9, 1,
     )
     coarse = coarse.reshape(2, win2, rows2 // ROWS, 2, ROWS, COLS, wide)
     coarse = coarse.transpose(0, 3, 2, 4, 1, 5, 6).reshape(levels, rows2, cols2, wide)

time: 115 us -> 102 us (0.89)
  waiting for transfers between devices: 31.1 us -> 13.9 us
  Pallas kernels: 46 us -> 58 us
  starting transfers between devices: 17.3 us -> 7.68 us
  local copies, waits for them, and re-layouts: 17.4 us -> 19.5 us
    ppermute x4 -> x2, waiting for transfers between devices: 20.9 us -> 6.01 us  [from_next(): return lax.ppermute(block, axis, pairs)]
    pallas_call x2, Pallas kernels: 46 us -> 58 us  [call(): pl.pallas_call(kernel, grid=(steps,), in_specs=[tokens] + whole, out_spec...]
    ppermute x3 -> x1, starting transfers between devices: 7.64 us -> 0.06 us  [from_last(): return lax.ppermute(block, axis, pairs)]
    unnamed x12 -> x16, local copies, waits for them, and re-layouts: 1.76 us -> 7.5 us
    another operation x3 -> x0, local copies, waits for them, and re-layouts: 4.05 us -> none  [call(): tokens = [low, segments.reshape(steps, own, width), high]]
    ppermute x3 -> x1, waiting for transfers between devices: 10.2 us -> 7.93 us  [from_last(): return lax.ppermute(block, axis, pairs)]
    ppermute x4 -> x2, starting transfers between devices: 9.62 us -> 7.63 us  [from_next(): return lax.ppermute(block, axis, pairs)]
    slice x2 -> x0, local copies, waits for them, and re-layouts: 1.64 us -> none  [call(): high = from_next(segments[:, 0], 'lat', False)]
  transfers between devices with their start and end apart: 7 -> 3, of which waited for: 6 -> 3; matrix products, arithmetic and copies ran while one was open for 6% -> 2% of each run, Pallas kernels for 0% -> 0%
where the time goes in v3:
time: 102 us
  Pallas kernels  58 us (57%)
  local copies, waits for them, and re-layouts  19.5 us (19%)
  waiting for transfers between devices  13.9 us (14%)
  starting transfers between devices  7.68 us (8%)
  other arithmetic  2.24 us (2%)
    pallas_call x2, Pallas kernels, call(): pl.pallas_call(kernel, grid=(steps,), in_specs=[tokens] + whole, out_spec...  58 us
    ppermute x1, waiting for transfers between devices, from_last(): return lax.ppermute(block, axis, pairs)  7.93 us
    ppermute x2, starting transfers between devices, from_next(): return lax.ppermute(block, axis, pairs)  7.63 us
    unnamed x16, local copies, waits for them, and re-layouts  7.5 us
    ppermute x2, waiting for transfers between devices, from_next(): return lax.ppermute(block, axis, pairs)  6.01 us
    transpose x2, local copies, waits for them, and re-layouts, shards(): split.transpose(0, 4, 2, 1, 3, 5, 6)  2.94 us
  transfers between devices with their start and end apart: 3, of which 3 were waited for; matrix products, arithmetic and copies ran while one was open for 2% of the time, Pallas kernels for 0%

profile of v3, /device:TPU:0, one launch (start us, length us, event | category | flops | bytes accessed | tf_op | source)
XLA Modules:
  0.0 101.6 jit_solution(3423300266885485200)
XLA Ops:
  0.0 1.0 %slice.31 = bf16[4,12,6,512]{3,2,1,0:T(8,128)(2,1)S(1)} slice(bf16[4,12,24,512]{3,2,1,0:T(8,128)(2,1)} %param.9), slice={[0:4], [0:12], [0:6], [0:512]} | slice | bytes 589824 | tf_op jit(solution)/shard_map/slice | solution.py:254
  1.0 4.5 %collective-permute-start = (bf16[4,12,6,512]{3,2,1,0:T(8,128)(2,1)S(1)}, bf16[4,12,6,512]{3,2,1,0:T(8,128)(2,1)S(1)}, u32[]{:S(2)}, u32[]{:S(2)}) collective-permute-start(bf16[4,12,6,512]{3,2,1,0:T(8,128)(2,1)S(1)} %slice.31), channel_id=1, source_target_pairs={{1,0},{2,1},{3,2},{4,3},{5,4},{6,5},{7,6},{0,7},{9,8},{10,9},{11,1... | collective-permute-start | bytes 884744 | tf_op jit(solution)/shard_map/ppermute | solution.py:230
  5.6 1.8 %slice.30 = bf16[4,12,18,512]{3,2,1,0:T(8,128)(2,1)S(1)} slice(bf16[4,12,24,512]{3,2,1,0:T(8,128)(2,1)} %param.9), slice={[0:4], [0:12], [6:24], [0:512]} | slice | bytes 1769472 | tf_op jit(solution)/shard_map/slice | solution.py:254
  7.4 3.5 %collective-permute-done = bf16[4,12,6,512]{3,2,1,0:T(8,128)(2,1)S(1)} collective-permute-done((bf16[4,12,6,512]{3,2,1,0:T(8,128)(2,1)S(1)}, bf16[4,12,6,512]{3,2,1,0:T(8,128)(2,1)S(1)}, u32[]{:S(2)}, u32[]{:S(2)}) %collective-permute-start) | collective-permute-done | bytes 294944 | tf_op jit(solution)/shard_map/ppermute | solution.py:230
  10.9 0.2 fusion.1
  11.2 0.9 copy.20
  12.1 1.3 %reshape.24 = bf16[2,2,4,3,2,12,512]{6,1,0,5,4,3,2:T(2,128)(2,1)} reshape(bf16[4,12,24,512]{3,0,2,1:T(4,128)(2,1)S(1)} %copy.20) | data formatting | bytes 2359296 | tf_op jit(solution)/shard_map/reshape | solution.py:256
  13.4 2.3 %copy.21 = bf16[2,2,4,2,3,12,512]{6,2,5,4,3,1,0:T(4,128)(2,1)S(1)} copy(bf16[2,2,4,2,3,12,512]{6,3,0,5,1,4,2:T(2,128)(2,1)} %bitcast.21) | data formatting | bytes 2359296 | tf_op jit(solution)/shard_map/transpose | solution.py:257
  15.8 0.2 copy.22.x_ref
  16.1 0.8 copy-done.6
  16.9 1.6 %copy-done.3 = bf16[2048,512]{1,0:T(8,128)(2,1)S(1)} copy-done((bf16[2048,512]{1,0:T(8,128)(2,1)S(1)}, bf16[2048,512]{1,0:T(8,128)(2,1)}, u32[]{:S(2)}) %copy-start.3) | copy-done | bytes 2097176
  18.5 1.4 %copy-done.5 = bf16[512,1536]{1,0:T(8,128)(2,1)S(1)} copy-done((bf16[512,1536]{1,0:T(8,128)(2,1)S(1)}, bf16[512,1536]{1,0:T(8,128)(2,1)}, u32[]{:S(2)}) %copy-start.5) | copy-done | bytes 1572888
  19.9 38.6 %shard_map.91 = bf16[4,72,1024]{2,1,0:T(8,128)(2,1)S(1)} custom-call(bf16[4,4,72,512]{3,2,1,0:T(8,128)(2,1)S(1)} %copy.22.x_ref, bf16[512,1536]{1,0:T(8,128)(2,1)S(1)} %copy-done.5, bf16[512,512]{1,0:T(8,128)(2,1)S(1)} %copy-done.6, bf16[512,2048]{1,0:T(8,128)(2,1)S(1)} %copy-done.2, bf16[2048,512]{1,0:T(8,128)(2,1)S(1)} %copy-done.3, ...), custom_call_target="tpu_custom_call" | custom-call | flops 14000000000 | bytes 20971520 | tf_op jit(solution)/shard_map/pallas_call | solution.py:206
  58.5 0.5 copy.23
  58.9 0.2 reshape.26
  59.1 0.6 copy.24
  59.8 0.2 reshape.27
  60.1 3.1 %collective-permute-start.1 = (bf16[4,6,3,1024]{3,0,2,1:T(4,128)(2,1)S(1)}, bf16[4,6,3,1024]{3,0,2,1:T(4,128)(2,1)S(1)}, u32[]{:S(2)}, u32[]{:S(2)}) collective-permute-start(bf16[4,6,3,1024]{3,0,2,1:T(4,128)(2,1)S(1)} %slice.43), channel_id=1, source_target_pairs={{1,0},{2,1},{3,2},{4,3},{5,4},{6,5},{7,6},{0,7},{9,8},{10,9},{11,1... | collective-permute-start | bytes 442376 | tf_op jit(solution)/shard_map/ppermute | solution.py:230
  63.3 2.5 %collective-permute-done.1 = bf16[4,6,3,1024]{3,0,2,1:T(4,128)(2,1)S(1)} collective-permute-done((bf16[4,6,3,1024]{3,0,2,1:T(4,128)(2,1)S(1)}, bf16[4,6,3,1024]{3,0,2,1:T(4,128)(2,1)S(1)}, u32[]{:S(2)}, u32[]{:S(2)}) %collective-permute-start.1) | collective-permute-done | bytes 147488 | tf_op jit(solution)/shard_map/ppermute | solution.py:230
  65.8 0.4 pad_maximum_fusion.2
  66.2 0.2 reshape.28
  66.4 0.6 copy.25
  67.2 0.8 copy-done.4
  68.0 2.8 %copy-done = bf16[1024,3072]{1,0:T(8,128)(2,1)S(1)} copy-done((bf16[1024,3072]{1,0:T(8,128)(2,1)S(1)}, bf16[1024,3072]{1,0:T(8,128)(2,1)}, u32[]{:S(2)}) %copy-start) | copy-done | bytes 6291480
  70.8 19.4 %shard_map.92 = bf16[2,144,1024]{2,1,0:T(8,128)(2,1)S(1)} custom-call(bf16[2,2,72,1024]{3,2,1,0:T(8,128)(2,1)S(1)} %copy.26.x_ref, bf16[1024,3072]{1,0:T(8,128)(2,1)S(1)} %copy-done, bf16[1024,1024]{1,0:T(8,128)(2,1)S(1)} %copy-done.4), custom_call_target="tpu_custom_call" | custom-call | flops 7000000000 | bytes 20971520 | tf_op jit(solution)/shard_map/pallas_call | solution.py:206
  90.2 0.6 copy.27
  90.9 0.6 copy.28
  91.5 0.2 reshape.31
  91.7 0.3 slice.44
  92.0 0.3 fusion.3
  92.4 7.9 %collective-permute-done.2 = bf16[4,6,6,1024]{3,0,2,1:T(4,128)(2,1)S(1)} collective-permute-done((bf16[4,6,6,1024]{3,0,2,1:T(4,128)(2,1)S(1)}, bf16[4,6,6,1024]{3,0,2,1:T(4,128)(2,1)S(1)}, u32[]{:S(2)}, u32[]{:S(2)}) %collective-permute-start.2) | collective-permute-done | bytes 294944 | tf_op jit(solution)/shard_map/ppermute | solution.py:236
  100.3 1.2 %fusion.2 = bf16[4,6,12,1024]{3,0,2,1:T(4,128)(2,1)} fusion(bf16[3,6,12,1024]{3,0,2,1:T(4,128)(2,1)S(1)} %bitcast.20, bf16[1,6,12,1024]{3,0,2,1:T(2,128)(2,1)S(1)} %slice.44, bf16[4,6,6,1024]{3,0,2,1:T(4,128)(2,1)S(1)} %collective-permute-done.2), kind=kLoop, calls=%fused_computation.6 | loop fusion | flops 1769472 | bytes 1474560 | tf_op jit(solution)/shard_map/concatenate | solution.py:280
  (16 shorter events, 0.7 us)
Async XLA Ops:
  1.0 9.8 %collective-permute-start = (bf16[4,12,6,512]{3,2,1,0:T(8,128)(2,1)S(1)}, bf16[4,12,6,512]{3,2,1,0:T(8,128)(2,1)S(1)}, u32[]{:S(2)}, u32[]{:S(2)}) collective-permute-start(bf16[4,12,6,512]{3,2,1,0:T(8,128)(2,1)S(1)} %slice.31), channel_id=1, source_target_pairs={{1,0},{2,1},{3,2},{4,3},{5,4},{6,5},{7,6},{0,7},{9,8},{10,9},{11,1... | collective-permute-start | bytes 884744 | tf_op jit(solution)/shard_map/ppermute | solution.py:230
  12.1 3.9 %copy-start.2 = (bf16[512,2048]{1,0:T(8,128)(2,1)S(1)}, bf16[512,2048]{1,0:T(8,128)(2,1)}, u32[]{:S(2)}) copy-start(bf16[512,2048]{1,0:T(8,128)(2,1)} %up_ref.1) | copy-start | bytes 6291460
  12.1 3.9 %copy-start.7 = (bf16[288,288]{1,0:T(8,128)(2,1)S(1)}, bf16[288,288]{1,0:T(8,128)(2,1)}, u32[]{:S(2)}) copy-start(bf16[288,288]{1,0:T(8,128)(2,1)} %constant.2.clone.pick_ref) | copy-start | bytes 497668
  13.4 2.7 %copy-start.1 = (bf16[2048,1024]{1,0:T(8,128)(2,1)S(1)}, bf16[2048,1024]{1,0:T(8,128)(2,1)}, u32[]{:S(2)}) copy-start(bf16[2048,1024]{1,0:T(8,128)(2,1)} %merge_ref.1) | copy-start | bytes 12582916
  15.7 1.1 %copy-start.6 = (bf16[512,512]{1,0:T(8,128)(2,1)S(1)}, bf16[512,512]{1,0:T(8,128)(2,1)}, u32[]{:S(2)}) copy-start(bf16[512,512]{1,0:T(8,128)(2,1)} %out_ref.2) | copy-start | bytes 1572868
  16.9 1.6 %copy-start.3 = (bf16[2048,512]{1,0:T(8,128)(2,1)S(1)}, bf16[2048,512]{1,0:T(8,128)(2,1)}, u32[]{:S(2)}) copy-start(bf16[2048,512]{1,0:T(8,128)(2,1)} %down_ref.1) | copy-start | bytes 6291460
  18.5 1.4 %copy-start.5 = (bf16[512,1536]{1,0:T(8,128)(2,1)S(1)}, bf16[512,1536]{1,0:T(8,128)(2,1)}, u32[]{:S(2)}) copy-start(bf16[512,1536]{1,0:T(8,128)(2,1)} %qkv_ref.2) | copy-start | bytes 4718596
  60.1 5.8 %collective-permute-start.1 = (bf16[4,6,3,1024]{3,0,2,1:T(4,128)(2,1)S(1)}, bf16[4,6,3,1024]{3,0,2,1:T(4,128)(2,1)S(1)}, u32[]{:S(2)}, u32[]{:S(2)}) collective-permute-start(bf16[4,6,3,1024]{3,0,2,1:T(4,128)(2,1)S(1)} %slice.43), channel_id=1, source_target_pairs={{1,0},{2,1},{3,2},{4,3},{5,4},{6,5},{7,6},{0,7},{9,8},{10,9},{11,1... | collective-permute-start | bytes 442376 | tf_op jit(solution)/shard_map/ppermute | solution.py:230
  66.4 1.6 %copy-start.4 = (bf16[1024,1024]{1,0:T(8,128)(2,1)S(1)}, bf16[1024,1024]{1,0:T(8,128)(2,1)}, u32[]{:S(2)}) copy-start(bf16[1024,1024]{1,0:T(8,128)(2,1)} %out_ref.3) | copy-start | bytes 6291460
  68.0 2.8 %copy-start = (bf16[1024,3072]{1,0:T(8,128)(2,1)S(1)}, bf16[1024,3072]{1,0:T(8,128)(2,1)}, u32[]{:S(2)}) copy-start(bf16[1024,3072]{1,0:T(8,128)(2,1)} %qkv_ref.3) | copy-start | bytes 18874372
  92.3 8.0 %collective-permute-start.2 = (bf16[4,6,6,1024]{3,0,2,1:T(4,128)(2,1)S(1)}, bf16[4,6,6,1024]{3,0,2,1:T(4,128)(2,1)S(1)}, u32[]{:S(2)}, u32[]{:S(2)}) collective-permute-start(bf16[4,6,6,1024]{3,0,2,1:T(4,128)(2,1)S(1)} %fusion.3), channel_id=1, source_target_pairs={{0,1},{1,2},{2,3},{3,4},{4,5},{5,6},{6,7},{7,0},{8,9},{9,10},{10,1... | collective-permute-start | bytes 884744 | tf_op jit(solution)/shard_map/ppermute | solution.py:236
